TPU v7x, 512 devices: a whole 4x4x16 slice. The times are simulated.
512 devices in a mesh: grid: 64 (over y_lo, z, core), member: 8 (over y_hi, x).
Axes of the slice: x: 4, y: 4 (y_hi: 2, y_lo: 2; y = y_hi * 2 + y_lo), z: 16, core: 2. Of those that a mesh axis runs over, the one named last changes fastest.
Arguments:
- states: bfloat16 [8, 65536, 1024], P('member', 'grid'), may hold values from -6 to 6
- weight: bfloat16 [1024, 100], replicated, may hold values from -0.1875 to 0.1875
- target: float32 [100, 65536], P(None, 'grid'), may hold values from -6 to 6
- area: float32 [65536], P('grid'), may hold values from 0.5 to 4.5
Outputs:
- loss: float32 [], replicated
- grad_states: bfloat16 [8, 65536, 1024], P('member', 'grid')
- grad_weight: float32 [1024, 100], replicated
All inputs are finite; a program needn't handle non-finite values.
Results may differ from a plain program's by a relative error of at most 0.0049.
Values may be sent and summed in bfloat16 or wider, within the bound.
No kernel may reach another device: no remote copies, remote signals or barrier semaphores. Data moves between devices by JAX's collectives and lax.ppermute only.
A program may use at most 64 MiB of HBM per device.

v0:
```python
import jax
import jax.numpy as jnp
from jax import lax
from jax.sharding import PartitionSpec as P

EPS_SQ = 0.0001


def smooth_abs(t):
    return jnp.sqrt(t * t + EPS_SQ)


def smooth_sign(t):
    return t / jnp.sqrt(t * t + EPS_SQ)


def shards(states, weight, target, area):
    local_states = states[0]
    members = lax.axis_size("member")
    points = local_states.shape[0]
    grid_total = points * lax.axis_size("grid")
    variables = weight.shape[1]
    coef = 1.0 / (members - 1)
    pred = lax.dot_general(
        weight, local_states, (((0,), (1,)), ((), ())), preferred_element_type=jnp.float32
    )
    everyone = lax.all_gather(pred[None], "member", axis=0, tiled=True)
    diff_t = pred - target
    delta = pred[None] - everyone
    pairsum = jnp.sum(smooth_abs(delta), axis=0)
    pairgrad = jnp.sum(smooth_sign(delta), axis=0)
    per = smooth_abs(diff_t) - 0.5 * coef * pairsum
    loss_local = jnp.sum(area[None, :] * per)
    dpred = (area[None, :] * (smooth_sign(diff_t) - coef * pairgrad)).astype(jnp.bfloat16)
    grad_local = lax.dot_general(
        dpred, weight, (((0,), (1,)), ((), ())), preferred_element_type=jnp.float32
    ).astype(jnp.bfloat16)
    wterm = lax.dot_general(
        local_states, dpred, (((0,), (1,)), ((), ())), preferred_element_type=jnp.float32
    )
    wsum, lsum = lax.psum((wterm, loss_local), ("grid", "member"))
    loss = lsum / (grid_total * variables * members)
    return (loss, grad_local[None], wsum / grid_total)


def solution(mesh):
    in_specs = (P("member", "grid", None), P(), P(None, "grid"), P("grid"))
    out_specs = (P(), P("member", "grid", None), P())
    return jax.shard_map(shards, mesh=mesh, in_specs=in_specs, out_specs=out_specs, check_vma=False)
```

profile of v0, /device:TPU:1, one launch (start us, length us, event | category | flops | bytes accessed | tf_op | source)
XLA Modules:
  0.0 569.6 jit_solution(10186914121408547995)
XLA Ops:
  7.2 0.0 copy-start
  7.2 0.0 copy-start.4
  7.2 0.0 copy-start.3
  7.2 0.0 all-gather.4.cloned.1.call-start
  7.2 1.5 copy-done
  8.8 2.5 fusion.5
  11.2 0.0 copy-start.1
  11.2 0.0 all-gather.4.cloned.1.call-update
  11.3 0.0 all-reduce.2.cloned.1.call-start
  11.3 86.1 %all-gather.4.cloned.1.call-done = f32[8,100,1024]{2,1,0:T(8,128)} async-done(((f32[1,100,1024]{2,1,0:T(8,128)}), f32[8,100,1024]{2,1,0:T(8,128)}) %all-gather.4.cloned.1.call-update) | async-done | bytes 3276816 | tf_op jit(solution)/shard_map/all_gather | solution.py:27
  97.4 4.0 fusion.2
  101.4 0.0 copy-start.2
  101.4 0.0 copy-done.4
  101.5 0.0 copy-done.3
  101.5 0.0 copy-done.1
  101.5 0.9 multiply_convert_fusion
  102.4 1.2 fusion.7
  103.6 0.0 all-reduce.2.cloned.1.call-update
  103.6 103.6 %psum.14 = f32[]{:T(128)} all-reduce(f32[]{:T(128)} %get-tuple-element.6), channel_id=1, replica_groups=mesh['grid'=64,'member'=8] {'grid','member'}, use_global_device_ids=true, to_apply=%region_2.0 | all-reduce | flops 1 | bytes 8 | tf_op jit(solution)/shard_map/psum | solution.py:41
  207.9 0.0 copy-done.2
  207.9 2.1 convert_bitcast_fusion
  209.9 349.9 %all-reduce.2.cloned.1.call-done = f32[1024,100]{0,1:T(8,128)} async-done(((f32[1024,100]{0,1:T(8,128)}), f32[1024,100]{0,1:T(8,128)}) %all-reduce.2.cloned.1.call-update) | async-done | bytes 409616 | tf_op jit(solution)/shard_map/psum | solution.py:41
  559.8 1.8 broadcast_multiply_fusion
Async XLA Ops:
  7.2 1.6 copy-start
  7.2 94.3 %copy-start.4 = (f32[1024]{0:T(1024)S(1)}, f32[1024]{0:T(1024)}, u32[]{:S(2)}) copy-start(f32[1024]{0:T(1024)} %param.7) | copy-start | bytes 12292
  7.2 94.3 %copy-start.3 = (f32[100,1024]{1,0:T(8,128)S(1)}, f32[100,1024]{1,0:T(8,128)}, u32[]{:S(2)}) copy-start(f32[100,1024]{1,0:T(8,128)} %param.6) | copy-start | bytes 1228804
  7.2 90.2 %all-gather.4.cloned.1.call-start = ((), (), s32[]{:S(2)}) async-start(), calls=%async_computation.1 | async-start | bytes 3833856 | tf_op jit(solution)/shard_map/all_gather | solution.py:27
  11.2 90.2 %copy-start.1 = (f32[100,1024]{1,0:T(8,128)S(1)}, f32[100,1024]{1,0:T(8,128)}, u32[]{:S(2)}) copy-start(f32[100,1024]{1,0:T(8,128)} %fusion.5) | copy-start | bytes 1228804
  11.3 548.5 %all-reduce.2.cloned.1.call-start = ((), (), s32[]{:S(2)}) async-start(), calls=%async_computation | async-start | bytes 851968 | tf_op jit(solution)/shard_map/psum | solution.py:41
  101.4 106.4 %copy-start.2 = (bf16[1024,100]{0,1:T(8,128)(2,1)S(1)}, bf16[1024,100]{0,1:T(8,128)(2,1)}, u32[]{:S(2)}) copy-start(bf16[1024,100]{0,1:T(8,128)(2,1)} %param.5) | copy-start | bytes 614404
Sparse Core Ops, SparseCore 0:
  11.8 85.5 all-gather.3
  103.7 456.0 all-reduce.1
where the time goes:
time: 571 us; the launch traced here: 570 us
  waiting for transfers between devices  436 us (76%)
  blocking collectives  104 us (18%)
  between operations  15.9 us (3%)
  other arithmetic  6.7 us (1%)
  matrix products  5.74 us (1%)
    psum x1, waiting for transfers between devices, shards(): wsum, lsum = lax.psum((wterm, loss_local), ('grid', 'member'))  350 us
    psum x1, blocking collectives, shards(): wsum, lsum = lax.psum((wterm, loss_local), ('grid', 'member'))  104 us
    all_gather x1, waiting for transfers between devices, shards(): everyone = lax.all_gather(pred[None], 'member', axis=0, tiled=True)  86.1 us
  transfers between devices with their start and end apart: 2, of which 2 were waited for; matrix products, arithmetic and copies ran while one was open for 0% of the time, Pallas kernels for 0%

commit v1 on v0

v1 whole, which is shorter than its diff:
```python
import jax
import jax.numpy as jnp
from jax import lax
from jax.sharding import Mesh, PartitionSpec as P

EPS_SQ = 0.0001
V = 100
VPAD = 128
MEMBER = ("y_hi", "x")
GRID = ("y_lo", "z", "core")
PLANE = ("y_lo", "core", "y_hi", "x")
WSCALE = 0.25
ZSCALE = 1.0 / 1024.0


def exchange(x, axes):
    return lax.all_to_all(x, axes, 0, 0, tiled=True)


def smooth_inverse(t):
    return lax.rsqrt(t * t + EPS_SQ)


def shards(states, weight, target, area):
    local_states = states[0]
    members = lax.axis_size(MEMBER)
    plane = lax.axis_size(PLANE)
    depth = lax.axis_size("z")
    points, width = local_states.shape
    grid_total = points * lax.axis_size(GRID)
    own = points // members
    coef = 1.0 / (members - 1)
    rank = lax.axis_index(MEMBER)
    pred = lax.dot_general(
        weight, local_states, (((0,), (1,)), ((), ())), preferred_element_type=jnp.float32
    )
    parts = pred.reshape(V, members, own).transpose(1, 0, 2)
    every = exchange(parts, MEMBER)
    goal = lax.dynamic_slice_in_dim(target, rank * own, own, 1)
    weights = lax.dynamic_slice_in_dim(area, rank * own, own, 0)
    diff = every - goal[None]
    inv = smooth_inverse(diff)
    sign = diff * inv
    size = (diff * diff + EPS_SQ) * inv
    signs, sizes = [], jnp.zeros((V, own), jnp.float32)
    for m in range(members):
        delta = every[m][None] - every
        inv = smooth_inverse(delta)
        signs.append(jnp.sum(delta * inv, axis=0))
        sizes = sizes + jnp.sum((delta * delta + EPS_SQ) * inv, axis=0)
    per = jnp.sum(size, axis=0) - 0.5 * coef * sizes
    loss = jnp.sum(weights[None] * per)
    dpart = (weights * (sign - coef * jnp.stack(signs))).astype(jnp.bfloat16)
    dpred = exchange(dpart, MEMBER).transpose(1, 0, 2).reshape(V, points)
    grad_local = lax.dot_general(
        dpred, weight, (((0,), (1,)), ((), ())), preferred_element_type=jnp.float32
    ).astype(jnp.bfloat16)
    wterm = lax.dot_general(
        dpred, local_states, (((1,), (0,)), ((), ())), preferred_element_type=jnp.float32
    )
    wterm = jnp.pad(wterm * WSCALE, ((0, VPAD - V), (0, 0)))
    groups = VPAD // 32
    chunks = wterm.reshape(groups, 32, width // 128, 128).transpose(0, 2, 1, 3)
    chunks = chunks.reshape(plane, 32, 128).astype(jnp.float16)
    scaled = loss * (1.0 / 65536.0)
    high = scaled.astype(jnp.float16)
    low = ((scaled - high.astype(jnp.float32)) * 1024.0).astype(jnp.float16)
    chunks = chunks.at[plane - 1, 31, 0].set(high)
    chunks = chunks.at[plane - 1, 31, 1].set(low)
    mine = jnp.sum(exchange(chunks, PLANE).astype(jnp.float32), axis=0)
    mine = (mine * (1.0 / 32.0)).astype(jnp.float16)
    ring = exchange(jnp.broadcast_to(mine[None], (depth, 32, 128)), "z")
    mine = jnp.sum(ring.astype(jnp.float32), axis=0)
    mine = (mine * (1.0 / 16.0)).astype(jnp.float16)
    whole = exchange(jnp.broadcast_to(mine[None], (plane, 32, 128)), PLANE)
    factor = 512.0 / WSCALE / grid_total
    table = whole.astype(jnp.float32)
    grads = table.reshape(groups, width // 128, 32, 128).transpose(0, 2, 1, 3)
    grads = grads.reshape(VPAD, width)[:V] * factor
    total = (table[plane - 1, 31, 0] + table[plane - 1, 31, 1] * (1.0 / 1024.0)) * (512.0 * 65536.0)
    return (total / (grid_total * V * members), grad_local[None], grads.T)


def solution(mesh):
    fine = Mesh(mesh.devices.reshape(2, 16, 2, 2, 4), GRID + MEMBER)
    in_specs = (P(MEMBER, GRID, None), P(), P(None, GRID), P(GRID))
    out_specs = (P(), P(MEMBER, GRID, None), P())
    return jax.shard_map(shards, mesh=fine, in_specs=in_specs, out_specs=out_specs, check_vma=False)
```

time: 571 us -> 99.1 us (0.17)
  waiting for transfers between devices: 436 us -> 19.9 us
  blocking collectives: 104 us -> 42.5 us
  starting transfers between devices: 0.08 us -> 18.2 us
  between operations: 15.9 us -> 3.99 us
    psum x1 -> x0, waiting for transfers between devices: 350 us -> none  [shards(): wsum, lsum = lax.psum((wterm, loss_local), ('grid', 'member'))]
    psum x1 -> x0, blocking collectives: 104 us -> none  [shards(): wsum, lsum = lax.psum((wterm, loss_local), ('grid', 'member'))]
    all_gather x1 -> x0, waiting for transfers between devices: 86.1 us -> none  [shards(): everyone = lax.all_gather(pred[None], 'member', axis=0, tiled=True)]
    all_to_all x0 -> x2, blocking collectives: none -> 42.5 us  [exchange(): return lax.all_to_all(x, axes, 0, 0, tiled=True)]
    all_to_all x0 -> x3, waiting for transfers between devices: none -> 19.9 us  [exchange(): return lax.all_to_all(x, axes, 0, 0, tiled=True)]
    all_to_all x0 -> x3, starting transfers between devices: none -> 18.2 us  [exchange(): return lax.all_to_all(x, axes, 0, 0, tiled=True)]
  transfers between devices with their start and end apart: 2 -> 3, of which waited for: 2 -> 3; matrix products, arithmetic and copies ran while one was open for 0% -> 4% of each run, Pallas kernels for 0% -> 0%
where the time goes in v1:
time: 99.1 us; the launch traced here: 98.5 us
  blocking collectives  42.5 us (43%)
  waiting for transfers between devices  19.9 us (20%)
  starting transfers between devices  18.2 us (18%)
  local copies, waits for them, and re-layouts  5.47 us (6%)
  matrix products  4.99 us (5%)
  between operations  3.99 us (4%)
  other arithmetic  3.45 us (3%)
    all_to_all x2, blocking collectives, exchange(): return lax.all_to_all(x, axes, 0, 0, tiled=True)  42.5 us
    all_to_all x3, waiting for transfers between devices, exchange(): return lax.all_to_all(x, axes, 0, 0, tiled=True)  19.9 us
    all_to_all x3, starting transfers between devices, exchange(): return lax.all_to_all(x, axes, 0, 0, tiled=True)  18.2 us
    dot_general x1, matrix products, shards(): lax.dot_general(weight, local_states, (((0,), (1,)), ((), ())), preferred...  2.47 us
    dot_general x1, matrix products, shards(): lax.dot_general(dpred, weight, (((0,), (1,)), ((), ())), preferred_elemen...  2.06 us
  transfers between devices with their start and end apart: 3, of which 3 were waited for; matrix products, arithmetic and copies ran while one was open for 4% of the time, Pallas kernels for 0%

profile of v1, /device:TPU:1, one launch (start us, length us, event | category | flops | bytes accessed | tf_op | source)
XLA Modules:
  0.0 98.5 jit_solution(7631511218981119554)
XLA Ops:
  0.6 0.0 copy-start
  0.6 1.6 %copy-done = bf16[1,1024,1024]{2,1,0:T(8,128)(2,1)S(1)} copy-done((bf16[1,1024,1024]{2,1,0:T(8,128)(2,1)S(1)}, bf16[1,1024,1024]{2,1,0:T(8,128)(2,1)}, u32[]{:S(2)}) %copy-start) | copy-done | bytes 2097176
  2.2 2.5 %convolution_bitcast_fusion = f32[8,100,128]{2,1,0:T(8,128)} fusion(bf16[8,128,1024]{2,1,0:T(8,128)(2,1)S(1)} %bitcast.75, bf16[1024,100]{0,1:T(8,128)(2,1)} %param.9), kind=kOutput, calls=%fused_computation.4 | convolution fusion | flops 209715200 | bytes 2711552 | tf_op jit(solution)/shard_map/dot_general | solution.py:34
  4.7 7.5 %all-to-all-start = ((f32[8,100,128]{2,1,0:T(8,128)}), f32[8,100,128]{2,1,0:T(8,128)S(1)}, u32[]{:S(2)}, u32[]{:S(2)}) async-start(f32[8,100,128]{2,1,0:T(8,128)} %convolution_bitcast_fusion), calls=%async_computation | async-start | bytes 851968 | tf_op jit(solution)/shard_map/all_to_all | solution.py:17
  12.2 0.8 dynamic_slice.6
  12.9 0.8 constant_dynamic-slice_fusion
  13.8 6.9 %all-to-all-done = f32[8,100,128]{2,1,0:T(8,128)S(1)} async-done(((f32[8,100,128]{2,1,0:T(8,128)}), f32[8,100,128]{2,1,0:T(8,128)S(1)}, u32[]{:S(2)}, u32[]{:S(2)}) %all-to-all-start) | async-done | bytes 409632 | tf_op jit(solution)/shard_map/all_to_all | solution.py:17
  20.7 1.0 %fusion.15 = (f32[100,128]{1,0:T(8,128)S(1)}, f32[100,128]{1,0:T(8,128)S(1)}, f32[100,128]{1,0:T(8,128)S(1)}, f32[100,128]{1,0:T(8,128)S(1)}, f32[100,128]{1,0:T...) fusion(f32[8,100,128]{2,1,0:T(8,128)S(1)} %all-to-all-done, ...), kind=kLoop, calls=%fused_computation.33 | loop fusion | flops 6028800 | bytes 1740800 | tf_op jit(solution)/shard_map/reduce_sum | solution.py:50
  21.9 0.8 fusion.10
  22.7 3.4 %all-to-all-start.1 = ((bf16[8,100,128]{2,1,0:T(8,128)(2,1)}), bf16[8,100,128]{2,1,0:T(8,128)(2,1)S(1)}, u32[]{:S(2)}, u32[]{:S(2)}) async-start(bf16[8,100,128]{2,1,0:T(8,128)(2,1)} %fusion.10), calls=%async_computation.1 | async-start | bytes 425984 | tf_op jit(solution)/shard_map/all_to_all | solution.py:17
  26.1 0.6 multiply_reduce_fusion
  27.4 6.0 %all-to-all-done.1 = bf16[8,100,128]{2,1,0:T(8,128)(2,1)S(1)} async-done(((bf16[8,100,128]{2,1,0:T(8,128)(2,1)}), bf16[8,100,128]{2,1,0:T(8,128)(2,1)S(1)}, u32[]{:S(2)}, u32[]{:S(2)}) %all-to-all-start.1) | async-done | bytes 204832 | tf_op jit(solution)/shard_map/all_to_all | solution.py:17
  33.5 0.5 fusion.5
  34.0 0.0 copy-start.1
  34.1 0.1 copy.16
  34.2 0.1 copy.13
  34.3 0.1 scatter.9
  34.4 16.8 %all_to_all.25 = f16[32,32,128]{2,1,0:T(8,128)(2,1)S(1)} all-to-all(f16[32,32,128]{2,1,0:T(8,128)(2,1)S(1)} %scatter.9), channel_id=1, replica_groups=mesh['y_lo'=2,'z'=16,'core'=2,'y_hi'=2,'x'=4] {'y_lo','core','y_hi','x'}, dimensions={0} | all-to-all | bytes 524288 | tf_op jit(solution)/shard_map/all_to_all | solution.py:17
  51.3 25.7 %all_to_all.26 = f16[16,32,128]{2,1,0:T(8,128)(2,1)S(1)} all-to-all(f16[16,32,128]{2,1,0:T(8,128)(2,1)S(1)} %broadcast_in_dim.6), channel_id=1, replica_groups=mesh['y_lo'=2,'z'=16,'core'=2,'y_hi'=2,'x'=4] {'z'}, dimensions={0} | all-to-all | bytes 262144 | tf_op jit(solution)/shard_map/all_to_all | solution.py:17
  77.1 0.7 broadcast_in_dim.7
  77.8 7.3 %all-to-all-start.4 = ((f16[32,32,128]{2,1,0:T(8,128)(2,1)}), f16[32,32,128]{2,1,0:T(8,128)(2,1)S(1)}, u32[]{:S(2)}, u32[]{:S(2)}) async-start(f16[32,32,128]{2,1,0:T(8,128)(2,1)} %broadcast_in_dim.7), calls=%async_computation.4 | async-start | bytes 524288 | tf_op jit(solution)/shard_map/all_to_all | solution.py:17
  85.2 0.0 copy-done.1
  85.2 2.1 %convert_bitcast_fusion = bf16[1,1024,1024]{2,1,0:T(8,128)(2,1)} fusion(bf16[100,1024]{1,0:T(8,128)(2,1)S(1)} %bitcast.79, bf16[1024,100]{0,1:T(8,128)(2,1)S(1)} %copy-done.1), kind=kOutput, calls=%fused_computation.2 | convolution fusion | flops 210763776 | bytes 2506752 | tf_op jit(solution)/shard_map/dot_general | solution.py:55
  87.2 6.9 %all-to-all-done.4 = f16[32,32,128]{2,1,0:T(8,128)(2,1)S(1)} async-done(((f16[32,32,128]{2,1,0:T(8,128)(2,1)}), f16[32,32,128]{2,1,0:T(8,128)(2,1)S(1)}, u32[]{:S(2)}, u32[]{:S(2)}) %all-to-all-start.4) | async-done | bytes 262176 | tf_op jit(solution)/shard_map/all_to_all | solution.py:17
  94.2 0.1 convert_element_type.61
  94.2 0.6 fusion.30
  94.8 0.3 copy.14
  95.1 0.1 copy.19
  95.2 0.8 fusion.28
  (19 shorter events, 0.4 us)
Async XLA Ops:
  0.6 1.6 %copy-start = (bf16[1,1024,1024]{2,1,0:T(8,128)(2,1)S(1)}, bf16[1,1024,1024]{2,1,0:T(8,128)(2,1)}, u32[]{:S(2)}) copy-start(bf16[1,1024,1024]{2,1,0:T(8,128)(2,1)} %param.8) | copy-start | bytes 6291460
  4.7 16.0 %all-to-all-start = ((f32[8,100,128]{2,1,0:T(8,128)}), f32[8,100,128]{2,1,0:T(8,128)S(1)}, u32[]{:S(2)}, u32[]{:S(2)}) async-start(f32[8,100,128]{2,1,0:T(8,128)} %convolution_bitcast_fusion), calls=%async_computation | async-start | bytes 851968 | tf_op jit(solution)/shard_map/all_to_all | solution.py:17
  22.7 10.7 %all-to-all-start.1 = ((bf16[8,100,128]{2,1,0:T(8,128)(2,1)}), bf16[8,100,128]{2,1,0:T(8,128)(2,1)S(1)}, u32[]{:S(2)}, u32[]{:S(2)}) async-start(bf16[8,100,128]{2,1,0:T(8,128)(2,1)} %fusion.10), calls=%async_computation.1 | async-start | bytes 425984 | tf_op jit(solution)/shard_map/all_to_all | solution.py:17
  34.0 51.2 %copy-start.1 = (bf16[1024,100]{0,1:T(8,128)(2,1)S(1)}, bf16[1024,100]{0,1:T(8,128)(2,1)}, u32[]{:S(2)}) copy-start(bf16[1024,100]{0,1:T(8,128)(2,1)} %param.9) | copy-start | bytes 614404
  77.8 16.3 %all-to-all-start.4 = ((f16[32,32,128]{2,1,0:T(8,128)(2,1)}), f16[32,32,128]{2,1,0:T(8,128)(2,1)S(1)}, u32[]{:S(2)}, u32[]{:S(2)}) async-start(f16[32,32,128]{2,1,0:T(8,128)(2,1)} %broadcast_in_dim.7), calls=%async_computation.4 | async-start | bytes 524288 | tf_op jit(solution)/shard_map/all_to_all | solution.py:17

commit v2 on v1

v2 whole, which is shorter than its diff:
```python
import jax
import jax.numpy as jnp
from jax import lax
from jax.experimental import pallas as pl
from jax.experimental.pallas import tpu as pltpu
from jax.sharding import Mesh, PartitionSpec as P

EPS_SQ = 0.0001
V = 100
VPAD = 128
BLOCK = 128
ROWS = 32
MEMBER = ("y_hi", "x")
GRID = ("y_lo", "z", "core")
PLANE = ("y_lo", "core", "y_hi", "x")
WSCALE = 0.25
LSCALE = 1.0 / 512.0
VMEM = pl.BlockSpec(memory_space=pltpu.VMEM)
SMEM = pl.BlockSpec(memory_space=pltpu.SMEM)


def exchange(x, axes):
    return lax.all_to_all(x, axes, 0, 0, tiled=True)


def pair_kernel(rank, diff, area, dpart, loss):
    members = diff.shape[0]
    coef = 1.0 / (members - 1)
    floor = coef * 0.5 * members * EPS_SQ**0.5
    weights = area[pl.ds(rank[0], 1), :]
    total = jnp.zeros((1, BLOCK), jnp.float32)
    for low in range(0, V, 16):
        high = min(low + 16, V)
        own = [diff[m, low:high, :] for m in range(members)]
        signs = [None] * members
        direct, size = None, None
        for m in range(members):
            square = own[m] * own[m] + EPS_SQ
            inv = lax.rsqrt(square)
            direct = square * inv if direct is None else direct + square * inv
            signs[m] = own[m] * inv
        pulls = [None] * members
        for i in range(members):
            for j in range(i + 1, members):
                delta = own[i] - own[j]
                square = delta * delta + EPS_SQ
                inv = lax.rsqrt(square)
                sign = delta * inv
                size = square * inv if size is None else size + square * inv
                pulls[i] = sign if pulls[i] is None else pulls[i] + sign
                pulls[j] = -sign if pulls[j] is None else pulls[j] - sign
        for m in range(members):
            dpart[m, low:high, :] = (weights * (signs[m] - coef * pulls[m])).astype(jnp.bfloat16)
        per = weights * (direct - coef * size - floor)
        total = total + jnp.sum(per, axis=0, keepdims=True)
    loss[...] = total


def pairs(rank, diff, area):
    return pl.pallas_call(
        pair_kernel,
        out_shape=(
            jax.ShapeDtypeStruct(diff.shape, jnp.bfloat16),
            jax.ShapeDtypeStruct((1, BLOCK), jnp.float32),
        ),
        in_specs=[SMEM, VMEM, VMEM],
        out_specs=(VMEM, VMEM),
        compiler_params=pltpu.CompilerParams(vmem_limit_bytes=8 * 1024 * 1024),
    )(rank, diff, area)


def finish_kernel(factor, loss_factor, table, grads, loss):
    columns = grads.shape[1] // BLOCK
    for g in range(VPAD // ROWS):
        rows = min(ROWS, V - g * ROWS)
        for c in range(columns):
            grads[g * ROWS : g * ROWS + rows, c * BLOCK : (c + 1) * BLOCK] = (
                table[g * columns + c, :rows, :] * factor
            )
    last = table.shape[0] - 1
    lanes = table[last, ROWS - 2 : ROWS - 1, :] + table[last, ROWS - 1 : ROWS, :] * (1.0 / 1024.0)
    loss[0, 0] = jnp.sum(lanes) * loss_factor


def finish(table, factor, loss_factor, width):
    return pl.pallas_call(
        lambda *refs: finish_kernel(factor, loss_factor, *refs),
        out_shape=(
            jax.ShapeDtypeStruct((V, width), jnp.float32),
            jax.ShapeDtypeStruct((1, 1), jnp.float32),
        ),
        in_specs=[VMEM],
        out_specs=(pl.BlockSpec((V, width), lambda: (0, 0)), SMEM),
        compiler_params=pltpu.CompilerParams(vmem_limit_bytes=8 * 1024 * 1024),
    )(table)


def shards(states, weight, target, area):
    members = lax.axis_size(MEMBER)
    plane = lax.axis_size(PLANE)
    depth = lax.axis_size("z")
    points, width = states.shape[1:]
    grid_total = points * lax.axis_size(GRID)
    rank = lax.axis_index(MEMBER)
    local_states = states[0]
    pred = lax.dot_general(
        weight, local_states, (((0,), (1,)), ((), ())), preferred_element_type=jnp.float32
    )
    diff = (pred - target).astype(jnp.float16).reshape(V, members, BLOCK).transpose(1, 0, 2)
    every = exchange(diff, MEMBER).astype(jnp.float32)
    dpart, loss = pairs(rank[None], every, area.reshape(members, BLOCK))
    dpred = exchange(dpart, MEMBER).transpose(1, 0, 2).reshape(V, points)
    grad_local = lax.dot_general(
        dpred, weight, (((0,), (1,)), ((), ())), preferred_element_type=jnp.float32
    ).astype(jnp.bfloat16)
    wterm = lax.dot_general(
        dpred, local_states, (((1,), (0,)), ((), ())), preferred_element_type=jnp.float32
    )
    scaled = loss * LSCALE
    top = scaled.astype(jnp.float16)
    rest = ((scaled - top.astype(jnp.float32)) * 1024.0).astype(jnp.float16)
    tail = jnp.concatenate([jnp.zeros((VPAD - V - 2, BLOCK), jnp.float16), top, rest])
    groups, columns = VPAD // ROWS, width // BLOCK
    wterm = jnp.concatenate([(wterm * WSCALE).astype(jnp.float16), jnp.tile(tail, (1, columns))])
    chunks = wterm.reshape(groups, ROWS, columns, BLOCK).transpose(0, 2, 1, 3)
    chunks = chunks.reshape(plane, ROWS, BLOCK)
    mine = jnp.sum(exchange(chunks, PLANE).astype(jnp.float32), axis=0)
    mine = (mine * (1.0 / plane)).astype(jnp.float16)
    ring = exchange(jnp.broadcast_to(mine[None], (depth, ROWS, BLOCK)), "z")
    mine = jnp.sum(ring.astype(jnp.float32), axis=0)
    mine = (mine * (1.0 / depth)).astype(jnp.float16)
    whole = exchange(jnp.broadcast_to(mine[None], (plane, ROWS, BLOCK)), PLANE)
    devices = plane * depth
    grads, total = finish(
        whole.astype(jnp.float32),
        devices / WSCALE / grid_total,
        devices / LSCALE / (grid_total * V * members),
        width,
    )
    return (total[0, 0], grad_local[None], grads.T)


def solution(mesh):
    fine = Mesh(mesh.devices.reshape(2, 16, 2, 2, 4), GRID + MEMBER)
    in_specs = (P(MEMBER, GRID, None), P(), P(None, GRID), P(GRID))
    out_specs = (P(), P(MEMBER, GRID, None), P())
    return jax.shard_map(shards, mesh=fine, in_specs=in_specs, out_specs=out_specs, check_vma=False)
```

time: 99.1 us -> 93 us (0.938)
  between operations: 3.99 us -> 0.82 us
  other arithmetic: 3.45 us -> 0.34 us
  Pallas kernels: 0 us -> 2.09 us
  local copies, waits for them, and re-layouts: 5.47 us -> 3.54 us
  waiting for transfers between devices: 19.9 us -> 21.4 us
    pallas_call x0 -> x2, Pallas kernels: none -> 2.09 us  [the longest x1 1.28 us: pairs(): pl.pallas_call(pair_kernel, out_shape=(jax.ShapeDtypeStruct(diff.shape, j...]
    reduce_sum x2 -> x0, other arithmetic: 1.69 us -> none  [the longest x1 1.05 us: shards(): sizes = sizes + jnp.sum((delta * delta + EPS_SQ) * inv, axis=0)]
    all_to_all x3, waiting for transfers between devices: 19.9 us -> 21.4 us  [exchange(): return lax.all_to_all(x, axes, 0, 0, tiled=True)]
    dynamic_slice x2 -> x0, local copies, waits for them, and re-layouts: 1.57 us -> none  [the longest x1 0.81 us: shards(): goal = lax.dynamic_slice_in_dim(target, rank * own, own, 1)]
  transfers between devices with their start and end apart: 3 -> 3, of which waited for: 3 -> 3; matrix products, arithmetic and copies ran while one was open for 4% -> 2% of each run, Pallas kernels for 0% -> 0%
where the time goes in v2:
time: 93 us; the launch traced here: 92.5 us
  blocking collectives  41.6 us (45%)
  waiting for transfers between devices  21.4 us (23%)
  starting transfers between devices  18.2 us (20%)
  matrix products  4.42 us (5%)
  local copies, waits for them, and re-layouts  3.54 us (4%)
  Pallas kernels  2.09 us (2%)
    all_to_all x2, blocking collectives, exchange(): return lax.all_to_all(x, axes, 0, 0, tiled=True)  41.6 us
    all_to_all x3, waiting for transfers between devices, exchange(): return lax.all_to_all(x, axes, 0, 0, tiled=True)  21.4 us
    all_to_all x3, starting transfers between devices, exchange(): return lax.all_to_all(x, axes, 0, 0, tiled=True)  18.2 us
    dot_general x1, matrix products, shards(): lax.dot_general(dpred, weight, (((0,), (1,)), ((), ())), preferred_elemen...  2.05 us
    dot_general x1, matrix products, shards(): lax.dot_general(weight, local_states, (((0,), (1,)), ((), ())), preferred...  1.91 us
  transfers between devices with their start and end apart: 3, of which 3 were waited for; matrix products, arithmetic and copies ran while one was open for 2% of the time, Pallas kernels for 0%

profile of v2, /device:TPU:1, one launch (start us, length us, event | category | flops | bytes accessed | tf_op | source)
XLA Modules:
  0.0 92.5 jit_solution(606286654512429589)
XLA Ops:
  0.6 0.0 copy-start
  0.6 1.6 %copy-done = bf16[1,1024,1024]{2,1,0:T(8,128)(2,1)S(1)} copy-done((bf16[1,1024,1024]{2,1,0:T(8,128)(2,1)S(1)}, bf16[1,1024,1024]{2,1,0:T(8,128)(2,1)}, u32[]{:S(2)}) %copy-start) | copy-done | bytes 2097176
  2.2 0.0 copy-start.1
  2.2 1.9 %fusion.13 = f16[100,1024]{1,0:T(8,128)(2,1)S(1)} fusion(f32[100,1024]{1,0:T(8,128)} %param.6, bf16[1024,100]{0,1:T(8,128)(2,1)} %param.5, bf16[1,1024,1024]{2,1,0:T(8,128)(2,1)S(1)} %copy-done), kind=kOutput, calls=%fused_computation.8 | convolution fusion | flops 209920000 | bytes 2916352 | tf_op jit(solution)/shard_map/dot_general | solution.py:106
  4.1 0.1 copy.13
  4.3 0.7 copy.18
  5.0 7.5 %all-to-all-start = ((f16[8,100,128]{2,1,0:T(8,128)(2,1)}), f16[8,100,128]{2,1,0:T(8,128)(2,1)S(1)}, u32[]{:S(2)}, u32[]{:S(2)}) async-start(f16[8,100,128]{2,1,0:T(8,128)(2,1)} %bitcast.42), calls=%async_computation | async-start | bytes 425984 | tf_op jit(solution)/shard_map/all_to_all | solution.py:23
  12.5 7.4 %all-to-all-done = f16[8,100,128]{2,1,0:T(8,128)(2,1)S(1)} async-done(((f16[8,100,128]{2,1,0:T(8,128)(2,1)}), f16[8,100,128]{2,1,0:T(8,128)(2,1)S(1)}, u32[]{:S(2)}, u32[]{:S(2)}) %all-to-all-start) | async-done | bytes 204832 | tf_op jit(solution)/shard_map/all_to_all | solution.py:23
  19.9 0.0 copy-done.1
  19.9 1.3 %shard_map.67 = (bf16[8,100,128]{2,1,0:T(8,128)(2,1)}, f32[1,128]{1,0:T(1,128)S(1)}) custom-call(s32[1]{0:T(128)} %bitcast.rank, f32[8,100,128]{2,1,0:T(8,128)S(1)} %convert_element_type.45.diff, f32[8,128]{1,0:T(8,128)S(1)} %bitcast.43), custom_call_target="tpu_custom_call" | custom-call | tf_op jit(solution)/shard_map/pallas_call | solution.py:60
  21.2 3.4 %all-to-all-start.1 = ((bf16[8,100,128]{2,1,0:T(8,128)(2,1)}), bf16[8,100,128]{2,1,0:T(8,128)(2,1)S(1)}, u32[]{:S(2)}, u32[]{:S(2)}) async-start(bf16[8,100,128]{2,1,0:T(8,128)(2,1)} %get-tuple-element.7), calls=%async_computation.1 | async-start | bytes 425984 | tf_op jit(solution)/shard_map/all_to_all | solution.py:23
  24.6 0.1 pad_maximum_fusion
  24.8 7.1 %all-to-all-done.1 = bf16[8,100,128]{2,1,0:T(8,128)(2,1)S(1)} async-done(((bf16[8,100,128]{2,1,0:T(8,128)(2,1)}), bf16[8,100,128]{2,1,0:T(8,128)(2,1)S(1)}, u32[]{:S(2)}, u32[]{:S(2)}) %all-to-all-start.1) | async-done | bytes 204832 | tf_op jit(solution)/shard_map/all_to_all | solution.py:23
  32.0 0.5 fusion.10
  32.5 0.0 copy-start.2
  32.5 0.1 maximum_bitcast_fusion
  32.6 0.1 copy.16
  32.7 0.1 copy.12
  32.8 16.7 %all_to_all.25 = f16[32,32,128]{2,1,0:T(8,128)(2,1)S(1)} all-to-all(f16[32,32,128]{2,1,0:T(8,128)(2,1)S(1)} %bitcast.47), channel_id=1, replica_groups=mesh['y_lo'=2,'z'=16,'core'=2,'y_hi'=2,'x'=4] {'y_lo','core','y_hi','x'}, dimensions={0} | all-to-all | bytes 524288 | tf_op jit(solution)/shard_map/all_to_all | solution.py:23
  49.6 24.9 %all_to_all.26 = f16[16,32,128]{2,1,0:T(8,128)(2,1)S(1)} all-to-all(f16[16,32,128]{2,1,0:T(8,128)(2,1)S(1)} %broadcast_in_dim.23), channel_id=1, replica_groups=mesh['y_lo'=2,'z'=16,'core'=2,'y_hi'=2,'x'=4] {'z'}, dimensions={0} | all-to-all | bytes 262144 | tf_op jit(solution)/shard_map/all_to_all | solution.py:23
  74.6 0.7 broadcast_in_dim.24
  75.3 7.3 %all-to-all-start.4 = ((f16[32,32,128]{2,1,0:T(8,128)(2,1)}), f16[32,32,128]{2,1,0:T(8,128)(2,1)S(1)}, u32[]{:S(2)}, u32[]{:S(2)}) async-start(f16[32,32,128]{2,1,0:T(8,128)(2,1)} %broadcast_in_dim.24), calls=%async_computation.4 | async-start | bytes 524288 | tf_op jit(solution)/shard_map/all_to_all | solution.py:23
  82.6 0.0 copy-done.2
  82.6 2.1 %convert_bitcast_fusion = bf16[1,1024,1024]{2,1,0:T(8,128)(2,1)} fusion(bf16[100,1024]{1,0:T(8,128)(2,1)S(1)} %bitcast.45, bf16[1024,100]{0,1:T(8,128)(2,1)S(1)} %copy-done.2), kind=kOutput, calls=%fused_computation.4 | convolution fusion | flops 210763776 | bytes 2506752 | tf_op jit(solution)/shard_map/dot_general | solution.py:113
  84.7 6.9 %all-to-all-done.4 = f16[32,32,128]{2,1,0:T(8,128)(2,1)S(1)} async-done(((f16[32,32,128]{2,1,0:T(8,128)(2,1)}), f16[32,32,128]{2,1,0:T(8,128)(2,1)S(1)}, u32[]{:S(2)}, u32[]{:S(2)}) %all-to-all-start.4) | async-done | bytes 262176 | tf_op jit(solution)/shard_map/all_to_all | solution.py:23
  91.6 0.1 convert_element_type.54.refs_0_
  91.7 0.8 shard_map.68
  (16 shorter events, 0.3 us)
Async XLA Ops:
  0.6 1.6 %copy-start = (bf16[1,1024,1024]{2,1,0:T(8,128)(2,1)S(1)}, bf16[1,1024,1024]{2,1,0:T(8,128)(2,1)}, u32[]{:S(2)}) copy-start(bf16[1,1024,1024]{2,1,0:T(8,128)(2,1)} %param.4) | copy-start | bytes 6291460
  2.2 17.7 %copy-start.1 = (f32[1024]{0:T(1024)S(1)}, f32[1024]{0:T(1024)}, u32[]{:S(2)}) copy-start(f32[1024]{0:T(1024)} %param.7) | copy-start | bytes 12292
  5.0 14.9 %all-to-all-start = ((f16[8,100,128]{2,1,0:T(8,128)(2,1)}), f16[8,100,128]{2,1,0:T(8,128)(2,1)S(1)}, u32[]{:S(2)}, u32[]{:S(2)}) async-start(f16[8,100,128]{2,1,0:T(8,128)(2,1)} %bitcast.42), calls=%async_computation | async-start | bytes 425984 | tf_op jit(solution)/shard_map/all_to_all | solution.py:23
  21.2 10.7 %all-to-all-start.1 = ((bf16[8,100,128]{2,1,0:T(8,128)(2,1)}), bf16[8,100,128]{2,1,0:T(8,128)(2,1)S(1)}, u32[]{:S(2)}, u32[]{:S(2)}) async-start(bf16[8,100,128]{2,1,0:T(8,128)(2,1)} %get-tuple-element.7), calls=%async_computation.1 | async-start | bytes 425984 | tf_op jit(solution)/shard_map/all_to_all | solution.py:23
  32.5 50.1 %copy-start.2 = (bf16[1024,100]{0,1:T(8,128)(2,1)S(1)}, bf16[1024,100]{0,1:T(8,128)(2,1)}, u32[]{:S(2)}) copy-start(bf16[1024,100]{0,1:T(8,128)(2,1)} %param.5) | copy-start | bytes 614404
  75.3 16.3 %all-to-all-start.4 = ((f16[32,32,128]{2,1,0:T(8,128)(2,1)}), f16[32,32,128]{2,1,0:T(8,128)(2,1)S(1)}, u32[]{:S(2)}, u32[]{:S(2)}) async-start(f16[32,32,128]{2,1,0:T(8,128)(2,1)} %broadcast_in_dim.24), calls=%async_computation.4 | async-start | bytes 524288 | tf_op jit(solution)/shard_map/all_to_all | solution.py:23

commit v3 on v2

--- a/solution.py
+++ b/solution.py
@@ -7,9 +7,8 @@
 
 EPS_SQ = 0.0001
 V = 100
-VPAD = 128
 BLOCK = 128
-ROWS = 32
+GROUPS = 4
 MEMBER = ("y_hi", "x")
 GRID = ("y_lo", "z", "core")
 PLANE = ("y_lo", "core", "y_hi", "x")
@@ -21,6 +20,29 @@
 
 def exchange(x, axes):
     return lax.all_to_all(x, axes, 0, 0, tiled=True)
+
+
+def project_kernel(states, weight, goal, diff):
+    for low in range(0, states.shape[0], 2 * BLOCK):
+        both = lax.dot_general(
+            weight[...],
+            states[low : low + 2 * BLOCK, :],
+            (((1,), (1,)), ((), ())),
+            preferred_element_type=jnp.float32,
+        )
+        for part in range(2):
+            r = low // BLOCK + part
+            diff[r] = both[:V, part * BLOCK : (part + 1) * BLOCK] - goal[r]
+
+
+def project(states, weight, goal):
+    return pl.pallas_call(
+        project_kernel,
+        out_shape=jax.ShapeDtypeStruct(goal.shape, jnp.float32),
+        in_specs=[VMEM, VMEM, VMEM],
+        out_specs=VMEM,
+        compiler_params=pltpu.CompilerParams(vmem_limit_bytes=8 * 1024 * 1024),
+    )(states, weight, goal)
 
 
 def pair_kernel(rank, diff, area, dpart, loss):
@@ -71,14 +93,13 @@
 
 def finish_kernel(factor, loss_factor, table, grads, loss):
     columns = grads.shape[1] // BLOCK
-    for g in range(VPAD // ROWS):
-        rows = min(ROWS, V - g * ROWS)
+    for g in range(GROUPS):
         for c in range(columns):
-            grads[g * ROWS : g * ROWS + rows, c * BLOCK : (c + 1) * BLOCK] = (
-                table[g * columns + c, :rows, :] * factor
-            )
-    last = table.shape[0] - 1
-    lanes = table[last, ROWS - 2 : ROWS - 1, :] + table[last, ROWS - 1 : ROWS, :] * (1.0 / 1024.0)
+            piece = table[g * columns + c] * factor
+            lanes = slice(c * BLOCK, (c + 1) * BLOCK)
+            grads[24 * g : 24 * (g + 1), lanes] = piece[:24]
+            grads[V - GROUPS + g : V - GROUPS + g + 1, lanes] = piece[24:25]
+    lanes = table[0, 25:26, :] + table[1, 25:26, :] * (1.0 / 1024.0)
     loss[0, 0] = jnp.sum(lanes) * loss_factor
 
 
@@ -103,12 +124,19 @@
     grid_total = points * lax.axis_size(GRID)
     rank = lax.axis_index(MEMBER)
     local_states = states[0]
-    pred = lax.dot_general(
-        weight, local_states, (((0,), (1,)), ((), ())), preferred_element_type=jnp.float32
-    )
-    diff = (pred - target).astype(jnp.float16).reshape(V, members, BLOCK).transpose(1, 0, 2)
+    columns = width // BLOCK
+    goal = lax.optimization_barrier(target.reshape(V, members, BLOCK).transpose(1, 0, 2))
+    diff = project(local_states, jnp.pad(weight.T, ((0, 28), (0, 0))), goal)
+    diff, rank = lax.optimization_barrier((diff.astype(jnp.float16), rank[None]))
     every = exchange(diff, MEMBER).astype(jnp.float32)
-    dpart, loss = pairs(rank[None], every, area.reshape(members, BLOCK))
+    dpart, loss = pairs(rank, every, area.reshape(members, BLOCK))
+    scaled = loss * LSCALE
+    top = scaled.astype(jnp.float16)
+    rest = ((scaled - top.astype(jnp.float32)) * 1024.0).astype(jnp.float16)
+    spare = jnp.concatenate([top, rest])[None, None]
+    spare = jnp.broadcast_to(spare, (GROUPS, columns // 2, 2, BLOCK))
+    spare = spare.reshape(GROUPS, columns, 1, BLOCK)
+    dpart, spare = lax.optimization_barrier((dpart, spare))
     dpred = exchange(dpart, MEMBER).transpose(1, 0, 2).reshape(V, points)
     grad_local = lax.dot_general(
         dpred, weight, (((0,), (1,)), ((), ())), preferred_element_type=jnp.float32
@@ -116,20 +144,17 @@
     wterm = lax.dot_general(
         dpred, local_states, (((1,), (0,)), ((), ())), preferred_element_type=jnp.float32
     )
-    scaled = loss * LSCALE
-    top = scaled.astype(jnp.float16)
-    rest = ((scaled - top.astype(jnp.float32)) * 1024.0).astype(jnp.float16)
-    tail = jnp.concatenate([jnp.zeros((VPAD - V - 2, BLOCK), jnp.float16), top, rest])
-    groups, columns = VPAD // ROWS, width // BLOCK
-    wterm = jnp.concatenate([(wterm * WSCALE).astype(jnp.float16), jnp.tile(tail, (1, columns))])
-    chunks = wterm.reshape(groups, ROWS, columns, BLOCK).transpose(0, 2, 1, 3)
-    chunks = chunks.reshape(plane, ROWS, BLOCK)
+    wterm = (wterm * WSCALE).astype(jnp.float16)
+    body = wterm[: V - GROUPS].reshape(GROUPS, 24, columns, BLOCK).transpose(0, 2, 1, 3)
+    last = wterm[V - GROUPS :].reshape(GROUPS, columns, 1, BLOCK)
+    chunks = jnp.concatenate([body, last, spare], axis=2).reshape(plane, 13, 2, BLOCK)
     mine = jnp.sum(exchange(chunks, PLANE).astype(jnp.float32), axis=0)
     mine = (mine * (1.0 / plane)).astype(jnp.float16)
-    ring = exchange(jnp.broadcast_to(mine[None], (depth, ROWS, BLOCK)), "z")
+    ring = exchange(jnp.broadcast_to(mine[None], (depth, 13, 2, BLOCK)), "z")
     mine = jnp.sum(ring.astype(jnp.float32), axis=0)
     mine = (mine * (1.0 / depth)).astype(jnp.float16)
-    whole = exchange(jnp.broadcast_to(mine[None], (plane, ROWS, BLOCK)), PLANE)
+    whole = exchange(jnp.broadcast_to(mine[None], (plane, 13, 2, BLOCK)), PLANE)
+    whole = whole.reshape(plane, 26, BLOCK)
     devices = plane * depth
     grads, total = finish(
         whole.astype(jnp.float32),

time: 93 us -> 88.4 us (0.951)
  blocking collectives: 41.6 us -> 65.6 us
  waiting for transfers between devices: 21.4 us -> 6.44 us
  starting transfers between devices: 18.2 us -> 6.43 us
  matrix products: 4.42 us -> 2.52 us
    all_to_all x2 -> x4, blocking collectives: 41.6 us -> 65.6 us  [exchange(): return lax.all_to_all(x, axes, 0, 0, tiled=True)]
    all_to_all x3 -> x1, waiting for transfers between devices: 21.4 us -> 6.44 us  [exchange(): return lax.all_to_all(x, axes, 0, 0, tiled=True)]
    all_to_all x3 -> x1, starting transfers between devices: 18.2 us -> 6.43 us  [exchange(): return lax.all_to_all(x, axes, 0, 0, tiled=True)]
    dot_general x1 -> x0, matrix products: 1.91 us -> none  [shards(): lax.dot_general(weight, local_states, (((0,), (1,)), ((), ())), preferred...]
  transfers between devices with their start and end apart: 3 -> 1, of which waited for: 3 -> 1; matrix products, arithmetic and copies ran while one was open for 2% -> 2% of each run, Pallas kernels for 0% -> 0%
where the time goes in v3:
time: 88.4 us; the launch traced here: 88.1 us
  blocking collectives  65.6 us (74%)
  waiting for transfers between devices  6.44 us (7%)
  starting transfers between devices  6.43 us (7%)
  local copies, waits for them, and re-layouts  3.48 us (4%)
  matrix products  2.52 us (3%)
  Pallas kernels  2.27 us (3%)
    all_to_all x4, blocking collectives, exchange(): return lax.all_to_all(x, axes, 0, 0, tiled=True)  65.6 us
    all_to_all x1, waiting for transfers between devices, exchange(): return lax.all_to_all(x, axes, 0, 0, tiled=True)  6.44 us
    all_to_all x1, starting transfers between devices, exchange(): return lax.all_to_all(x, axes, 0, 0, tiled=True)  6.43 us
    dot_general x1, matrix products, shards(): lax.dot_general(dpred, weight, (((0,), (1,)), ((), ())), preferred_elemen...  2.06 us
    unnamed x13, local copies, waits for them, and re-layouts  1.84 us
  transfers between devices with their start and end apart: 1, of which 1 were waited for; matrix products, arithmetic and copies ran while one was open for 2% of the time, Pallas kernels for 0%

profile of v3, /device:TPU:1, one launch (start us, length us, event | category | flops | bytes accessed | tf_op | source)
XLA Modules:
  0.0 88.1 jit_solution(16060489937119630024)
XLA Ops:
  0.6 0.0 copy-start.2
  0.6 0.0 copy-start
  0.7 1.2 %copy.38 = f32[13,8,8,128]{3,2,1,0:T(8,128)S(1)} copy(f32[13,8,8,128]{3,1,2,0:T(8,128)} %bitcast.56) | data formatting | bytes 851968
  1.9 0.1 copy.46
  2.0 0.0 copy-done.2
  2.1 0.4 copy-done
  2.5 0.0 copy-start.1
  2.5 0.8 shard_map.67
  3.4 14.7 %all_to_all.25 = f16[8,100,128]{2,1,0:T(8,128)(2,1)S(1)} all-to-all(f16[8,100,128]{2,1,0:T(8,128)(2,1)S(1)} %convert_element_type.48), channel_id=1, replica_groups=mesh['y_lo'=2,'z'=16,'core'=2,'y_hi'=2,'x'=4] {'y_hi','x'}, dimensions={0} | all-to-all | bytes 409600 | tf_op jit(solution)/shard_map/all_to_all | solution.py:22
  18.1 0.0 copy-done.1
  18.1 0.6 shard_map.68
  18.7 9.9 %all_to_all.26 = bf16[8,100,128]{2,1,0:T(8,128)(2,1)S(1)} all-to-all(bf16[8,100,128]{2,1,0:T(8,128)(2,1)S(1)} %get-tuple-element.15), channel_id=1, replica_groups=mesh['y_lo'=2,'z'=16,'core'=2,'y_hi'=2,'x'=4] {'y_hi','x'}, dimensions={0} | all-to-all | bytes 409600 | tf_op jit(solution)/shard_map/all_to_all | solution.py:22
  28.8 0.5 fusion
  29.3 0.1 copy.40
  29.4 0.1 pad_maximum_fusion
  29.5 0.3 copy.34
  29.8 15.5 %all_to_all.27 = f16[32,13,2,128]{3,2,1,0:T(2,128)(2,1)S(1)} all-to-all(f16[32,13,2,128]{3,2,1,0:T(2,128)(2,1)S(1)} %copy.34), channel_id=1, replica_groups=mesh['y_lo'=2,'z'=16,'core'=2,'y_hi'=2,'x'=4] {'y_lo','core','y_hi','x'}, dimensions={0} | all-to-all | bytes 425984 | tf_op jit(solution)/shard_map/all_to_all | solution.py:22
  45.3 0.2 convert_reduce_fusion
  45.5 0.1 broadcast_in_dim.32
  45.5 25.5 %all_to_all.28 = f16[16,13,2,128]{3,2,1,0:T(2,128)(2,1)S(1)} all-to-all(f16[16,13,2,128]{3,2,1,0:T(2,128)(2,1)S(1)} %broadcast_in_dim.32), channel_id=1, replica_groups=mesh['y_lo'=2,'z'=16,'core'=2,'y_hi'=2,'x'=4] {'z'}, dimensions={0} | all-to-all | bytes 212992 | tf_op jit(solution)/shard_map/all_to_all | solution.py:22
  71.1 0.1 convert_reduce_fusion.1
  71.1 0.8 broadcast_in_dim.33
  71.9 6.4 %all-to-all-start.4 = ((f16[32,13,2,128]{3,2,1,0:T(2,128)(2,1)}), f16[32,13,2,128]{3,2,1,0:T(2,128)(2,1)S(1)}, u32[]{:S(2)}, u32[]{:S(2)}) async-start(f16[32,13,2,128]{3,2,1,0:T(2,128)(2,1)} %broadcast_in_dim.33), calls=%async_computation.4 | async-start | bytes 425984 | tf_op jit(solution)/shard_map/all_to_all | solution.py:22
  78.4 2.1 %convert_bitcast_fusion = bf16[1,1024,1024]{2,1,0:T(8,128)(2,1)} fusion(bf16[100,1024]{1,0:T(8,128)(2,1)S(1)} %bitcast.49, bf16[1024,100]{0,1:T(8,128)(2,1)S(1)} %copy-done.2), kind=kOutput, calls=%fused_computation | convolution fusion | flops 210763776 | bytes 2506752 | tf_op jit(solution)/shard_map/dot_general | solution.py:141
  80.4 6.4 %all-to-all-done.4 = f16[32,13,2,128]{3,2,1,0:T(2,128)(2,1)S(1)} async-done(((f16[32,13,2,128]{3,2,1,0:T(2,128)(2,1)}), f16[32,13,2,128]{3,2,1,0:T(2,128)(2,1)S(1)}, u32[]{:S(2)}, u32[]{:S(2)}) %all-to-all-start.4) | async-done | bytes 213024 | tf_op jit(solution)/shard_map/all_to_all | solution.py:22
  86.9 0.1 copy.36
  86.9 0.1 bitcast_convert_fusion
  87.0 0.3 copy.37.refs_0_
  87.3 0.8 shard_map.69
  (17 shorter events, 0.3 us)
Async XLA Ops:
  0.6 1.4 %copy-start.2 = (bf16[1024,100]{0,1:T(8,128)(2,1)S(1)}, bf16[1024,100]{0,1:T(8,128)(2,1)}, u32[]{:S(2)}) copy-start(bf16[1024,100]{0,1:T(8,128)(2,1)} %param.5) | copy-start | bytes 614404
  0.6 1.8 %copy-start = (bf16[1,1024,1024]{2,1,0:T(8,128)(2,1)S(1)}, bf16[1,1024,1024]{2,1,0:T(8,128)(2,1)}, u32[]{:S(2)}) copy-start(bf16[1,1024,1024]{2,1,0:T(8,128)(2,1)} %param.4) | copy-start | bytes 6291460
  2.5 15.6 %copy-start.1 = (f32[1024]{0:T(1024)S(1)}, f32[1024]{0:T(1024)}, u32[]{:S(2)}) copy-start(f32[1024]{0:T(1024)} %param.7) | copy-start | bytes 12292
  71.9 14.9 %all-to-all-start.4 = ((f16[32,13,2,128]{3,2,1,0:T(2,128)(2,1)}), f16[32,13,2,128]{3,2,1,0:T(2,128)(2,1)S(1)}, u32[]{:S(2)}, u32[]{:S(2)}) async-start(f16[32,13,2,128]{3,2,1,0:T(2,128)(2,1)} %broadcast_in_dim.33), calls=%async_computation.4 | async-start | bytes 425984 | tf_op jit(solution)/shard_map/all_to_all | solution.py:22

commit v4 on v3

--- a/solution.py
+++ b/solution.py
@@ -1,3 +1,5 @@
+import itertools
+
 import jax
 import jax.numpy as jnp
 from jax import lax
@@ -11,15 +13,29 @@
 GROUPS = 4
 MEMBER = ("y_hi", "x")
 GRID = ("y_lo", "z", "core")
-PLANE = ("y_lo", "core", "y_hi", "x")
+PLANE = ("y_hi", "y_lo", "x", "core")
+MEMBER_FIRST = (1, 2)
+PLANE_FIRST = (1, 0, 2, 0)
+Z_FIRST = (8,)
 WSCALE = 0.25
 LSCALE = 1.0 / 512.0
 VMEM = pl.BlockSpec(memory_space=pltpu.VMEM)
 SMEM = pl.BlockSpec(memory_space=pltpu.SMEM)
 
 
-def exchange(x, axes):
-    return lax.all_to_all(x, axes, 0, 0, tiled=True)
+def places(axes, first):
+    sizes = [lax.axis_size(a) for a in axes]
+    order = []
+    for place in itertools.product(*map(range, sizes)):
+        index = 0
+        for step, begin, size in zip(place, first, sizes):
+            index = index * size + (begin + step) % size
+        order.append(index)
+    return order
+
+
+def exchange(x, axes, first):
+    return lax.all_to_all(x, axes, 0, 0, axis_index_groups=[places(axes, first)], tiled=True)
 
 
 def project_kernel(states, weight, goal, diff):
@@ -122,13 +138,16 @@
     depth = lax.axis_size("z")
     points, width = states.shape[1:]
     grid_total = points * lax.axis_size(GRID)
-    rank = lax.axis_index(MEMBER)
+    rank = 0
+    for axis, begin in zip(MEMBER, MEMBER_FIRST):
+        size = lax.axis_size(axis)
+        rank = rank * size + (lax.axis_index(axis) + size - begin) % size
     local_states = states[0]
     columns = width // BLOCK
     goal = lax.optimization_barrier(target.reshape(V, members, BLOCK).transpose(1, 0, 2))
     diff = project(local_states, jnp.pad(weight.T, ((0, 28), (0, 0))), goal)
     diff, rank = lax.optimization_barrier((diff.astype(jnp.float16), rank[None]))
-    every = exchange(diff, MEMBER).astype(jnp.float32)
+    every = exchange(diff, MEMBER, MEMBER_FIRST).astype(jnp.float32)
     dpart, loss = pairs(rank, every, area.reshape(members, BLOCK))
     scaled = loss * LSCALE
     top = scaled.astype(jnp.float16)
@@ -137,7 +156,7 @@
     spare = jnp.broadcast_to(spare, (GROUPS, columns // 2, 2, BLOCK))
     spare = spare.reshape(GROUPS, columns, 1, BLOCK)
     dpart, spare = lax.optimization_barrier((dpart, spare))
-    dpred = exchange(dpart, MEMBER).transpose(1, 0, 2).reshape(V, points)
+    dpred = exchange(dpart, MEMBER, MEMBER_FIRST).transpose(1, 0, 2).reshape(V, points)
     grad_local = lax.dot_general(
         dpred, weight, (((0,), (1,)), ((), ())), preferred_element_type=jnp.float32
     ).astype(jnp.bfloat16)
@@ -148,12 +167,12 @@
     body = wterm[: V - GROUPS].reshape(GROUPS, 24, columns, BLOCK).transpose(0, 2, 1, 3)
     last = wterm[V - GROUPS :].reshape(GROUPS, columns, 1, BLOCK)
     chunks = jnp.concatenate([body, last, spare], axis=2).reshape(plane, 13, 2, BLOCK)
-    mine = jnp.sum(exchange(chunks, PLANE).astype(jnp.float32), axis=0)
+    mine = jnp.sum(exchange(chunks, PLANE, PLANE_FIRST).astype(jnp.float32), axis=0)
     mine = (mine * (1.0 / plane)).astype(jnp.float16)
-    ring = exchange(jnp.broadcast_to(mine[None], (depth, 13, 2, BLOCK)), "z")
+    ring = exchange(jnp.broadcast_to(mine[None], (depth, 13, 2, BLOCK)), ("z",), Z_FIRST)
     mine = jnp.sum(ring.astype(jnp.float32), axis=0)
     mine = (mine * (1.0 / depth)).astype(jnp.float16)
-    whole = exchange(jnp.broadcast_to(mine[None], (plane, 13, 2, BLOCK)), PLANE)
+    whole = exchange(jnp.broadcast_to(mine[None], (plane, 13, 2, BLOCK)), PLANE, PLANE_FIRST)
     whole = whole.reshape(plane, 26, BLOCK)
     devices = plane * depth
     grads, total = finish(

time: 88.4 us -> 81 us (0.916)
  blocking collectives: 65.6 us -> 60.2 us
  waiting for transfers between devices: 6.44 us -> 1.53 us
  starting transfers between devices: 6.43 us -> 9.35 us
    all_to_all x4, blocking collectives: 65.6 us -> 60.2 us  [exchange(): lax.all_to_all(x, axes, 0, 0, axis_index_groups=[places(axes, first)], ti...]
    all_to_all x1, waiting for transfers between devices: 6.44 us -> 1.53 us  [exchange(): lax.all_to_all(x, axes, 0, 0, axis_index_groups=[places(axes, first)], ti...]
    all_to_all x1, starting transfers between devices: 6.43 us -> 9.35 us  [exchange(): lax.all_to_all(x, axes, 0, 0, axis_index_groups=[places(axes, first)], ti...]
  transfers between devices with their start and end apart: 1 -> 1, of which waited for: 1 -> 1; matrix products, arithmetic and copies ran while one was open for 2% -> 3% of each run, Pallas kernels for 0% -> 0%
where the time goes in v4:
time: 81 us; the launch traced here: 80.7 us
  blocking collectives  60.2 us (74%)
  starting transfers between devices  9.35 us (12%)
  local copies, waits for them, and re-layouts  3.46 us (4%)
  matrix products  2.52 us (3%)
  Pallas kernels  2.27 us (3%)
  waiting for transfers between devices  1.53 us (2%)
  between operations  0.9 us (1%)
    all_to_all x4, blocking collectives, exchange(): lax.all_to_all(x, axes, 0, 0, axis_index_groups=[places(axes, first)], ti...  60.2 us
    all_to_all x1, starting transfers between devices, exchange(): lax.all_to_all(x, axes, 0, 0, axis_index_groups=[places(axes, first)], ti...  9.35 us
    dot_general x1, matrix products, shards(): lax.dot_general(dpred, weight, (((0,), (1,)), ((), ())), preferred_elemen...  2.05 us
    unnamed x13, local copies, waits for them, and re-layouts  1.82 us
  transfers between devices with their start and end apart: 1, of which 1 were waited for; matrix products, arithmetic and copies ran while one was open for 3% of the time, Pallas kernels for 0%

profile of v4, /device:TPU:1, one launch (start us, length us, event | category | flops | bytes accessed | tf_op | source)
XLA Modules:
  0.0 80.7 jit_solution(15568145551709972029)
XLA Ops:
  0.6 0.0 copy-start.2
  0.6 0.0 copy-start
  0.7 1.2 %copy.38 = f32[13,8,8,128]{3,2,1,0:T(8,128)S(1)} copy(f32[13,8,8,128]{3,1,2,0:T(8,128)} %bitcast.56) | data formatting | bytes 851968
  1.9 0.1 copy.46
  2.0 0.0 copy-done.2
  2.1 0.4 copy-done
  2.5 0.0 copy-start.1
  2.5 0.8 %shard_map.67 = f32[8,100,128]{2,1,0:T(8,128)S(1)} custom-call(bf16[1024,1024]{1,0:T(8,128)(2,1)S(1)} %bitcast.45, bf16[128,1024]{1,0:T(8,128)(2,1)S(1)} %pad.4.weight, f32[8,100,128]{2,1,0:T(8,128)S(1)} %bitcast.46), custom_call_target="tpu_custom_call" | custom-call | tf_op jit(solution)/shard_map/pallas_call | solution.py:55
  3.4 11.2 %all_to_all.25 = f16[8,100,128]{2,1,0:T(8,128)(2,1)S(1)} all-to-all(f16[8,100,128]{2,1,0:T(8,128)(2,1)S(1)} %convert_element_type.48), channel_id=1, replica_groups={{6,7,4,5,2,3,0,1},{14,15,12,13,10,11,8,9},{22,23,20,21,18,19,16,17},{30..., dimensions={0} | all-to-all | bytes 409600 | tf_op jit(solution)/shard_map/all_to_all | solution.py:38
  14.6 0.0 copy-done.1
  14.6 0.6 shard_map.68
  15.3 9.6 %all_to_all.26 = bf16[8,100,128]{2,1,0:T(8,128)(2,1)S(1)} all-to-all(bf16[8,100,128]{2,1,0:T(8,128)(2,1)S(1)} %get-tuple-element.15), channel_id=1, replica_groups={{6,7,4,5,2,3,0,1},{14,15,12,13,10,11,8,9},{22,23,20,21,18,19,16,17},{30..., dimensions={0} | all-to-all | bytes 409600 | tf_op jit(solution)/shard_map/all_to_all | solution.py:38
  25.0 0.5 fusion
  25.5 0.1 copy.40
  25.7 0.1 pad_maximum_fusion
  25.7 0.3 copy.34
  26.0 18.6 %all_to_all.27 = f16[32,13,2,128]{3,2,1,0:T(2,128)(2,1)S(1)} all-to-all(f16[32,13,2,128]{3,2,1,0:T(2,128)(2,1)S(1)} %copy.34), channel_id=1, replica_groups={{6,14,7,15,4,12,5,13,262,270,263,271,260,268,261,269,2,10,3,11,0,8,1,9,..., dimensions={0} | all-to-all | bytes 425984 | tf_op jit(solution)/shard_map/all_to_all | solution.py:38
  44.6 0.2 convert_reduce_fusion
  44.8 0.1 broadcast_in_dim.32
  44.8 20.8 %all_to_all.28 = f16[16,13,2,128]{3,2,1,0:T(2,128)(2,1)S(1)} all-to-all(f16[16,13,2,128]{3,2,1,0:T(2,128)(2,1)S(1)} %broadcast_in_dim.32), channel_id=1, replica_groups={{128,144,160,176,192,208,224,240,0,16,32,48,64,80,96,112},{129,145,161,..., dimensions={0} | all-to-all | bytes 212992 | tf_op jit(solution)/shard_map/all_to_all | solution.py:38
  65.6 0.1 convert_reduce_fusion.1
  65.7 0.8 broadcast_in_dim.33
  66.5 9.3 %all-to-all-start.4 = ((f16[32,13,2,128]{3,2,1,0:T(2,128)(2,1)}), f16[32,13,2,128]{3,2,1,0:T(2,128)(2,1)S(1)}, u32[]{:S(2)}, u32[]{:S(2)}) async-start(f16[32,13,2,128]{3,2,1,0:T(2,128)(2,1)} %broadcast_in_dim.33), calls=%async_computation.4 | async-start | bytes 425984 | tf_op jit(solution)/shard_map/all_to_all | solution.py:38
  75.9 2.1 %convert_bitcast_fusion = bf16[1,1024,1024]{2,1,0:T(8,128)(2,1)} fusion(bf16[100,1024]{1,0:T(8,128)(2,1)S(1)} %bitcast.49, bf16[1024,100]{0,1:T(8,128)(2,1)S(1)} %copy-done.2), kind=kOutput, calls=%fused_computation | convolution fusion | flops 210763776 | bytes 2506752 | tf_op jit(solution)/shard_map/dot_general | solution.py:160
  77.9 1.5 %all-to-all-done.4 = f16[32,13,2,128]{3,2,1,0:T(2,128)(2,1)S(1)} async-done(((f16[32,13,2,128]{3,2,1,0:T(2,128)(2,1)}), f16[32,13,2,128]{3,2,1,0:T(2,128)(2,1)S(1)}, u32[]{:S(2)}, u32[]{:S(2)}) %all-to-all-start.4) | async-done | bytes 213024 | tf_op jit(solution)/shard_map/all_to_all | solution.py:38
  79.5 0.1 copy.36
  79.5 0.1 bitcast_convert_fusion
  79.6 0.3 copy.37.refs_0_
  79.9 0.8 %shard_map.69 = (f32[100,1024]{1,0:T(8,128)}, f32[1,1]{1,0:T(1,128)}) custom-call(f32[32,26,128]{2,1,0:T(8,128)S(1)} %copy.37.refs_0_), custom_call_target="tpu_custom_call" | custom-call | tf_op jit(solution)/shard_map/pallas_call | solution.py:123
  (17 shorter events, 0.3 us)
Async XLA Ops:
  0.6 1.4 %copy-start.2 = (bf16[1024,100]{0,1:T(8,128)(2,1)S(1)}, bf16[1024,100]{0,1:T(8,128)(2,1)}, u32[]{:S(2)}) copy-start(bf16[1024,100]{0,1:T(8,128)(2,1)} %param.5) | copy-start | bytes 614404
  0.6 1.8 %copy-start = (bf16[1,1024,1024]{2,1,0:T(8,128)(2,1)S(1)}, bf16[1,1024,1024]{2,1,0:T(8,128)(2,1)}, u32[]{:S(2)}) copy-start(bf16[1,1024,1024]{2,1,0:T(8,128)(2,1)} %param.4) | copy-start | bytes 6291460
  2.5 12.1 %copy-start.1 = (f32[1024]{0:T(1024)S(1)}, f32[1024]{0:T(1024)}, u32[]{:S(2)}) copy-start(f32[1024]{0:T(1024)} %param.7) | copy-start | bytes 12292
  66.5 12.9 %all-to-all-start.4 = ((f16[32,13,2,128]{3,2,1,0:T(2,128)(2,1)}), f16[32,13,2,128]{3,2,1,0:T(2,128)(2,1)S(1)}, u32[]{:S(2)}, u32[]{:S(2)}) async-start(f16[32,13,2,128]{3,2,1,0:T(2,128)(2,1)} %broadcast_in_dim.33), calls=%async_computation.4 | async-start | bytes 425984 | tf_op jit(solution)/shard_map/all_to_all | solution.py:38

commit v5 on v4

--- a/solution.py
+++ b/solution.py
@@ -15,7 +15,7 @@
 GRID = ("y_lo", "z", "core")
 PLANE = ("y_hi", "y_lo", "x", "core")
 MEMBER_FIRST = (1, 2)
-PLANE_FIRST = (1, 0, 2, 0)
+PLANE_FIRST = (1, 1, 2, 1)
 Z_FIRST = (8,)
 WSCALE = 0.25
 LSCALE = 1.0 / 512.0

time: 81 us -> 79.6 us (0.983)
  blocking collectives: 60.2 us -> 58.7 us
    all_to_all x4, blocking collectives: 60.2 us -> 58.7 us  [exchange(): lax.all_to_all(x, axes, 0, 0, axis_index_groups=[places(axes, first)], ti...]
where the time goes in v5:
time: 79.6 us; the launch traced here: 79.2 us
  blocking collectives  58.7 us (74%)
  starting transfers between devices  8.97 us (11%)
  local copies, waits for them, and re-layouts  3.46 us (4%)
  matrix products  2.52 us (3%)
  Pallas kernels  2.27 us (3%)
  waiting for transfers between devices  1.94 us (2%)
  between operations  0.9 us (1%)
    all_to_all x4, blocking collectives, exchange(): lax.all_to_all(x, axes, 0, 0, axis_index_groups=[places(axes, first)], ti...  58.7 us
    all_to_all x1, starting transfers between devices, exchange(): lax.all_to_all(x, axes, 0, 0, axis_index_groups=[places(axes, first)], ti...  8.97 us
    dot_general x1, matrix products, shards(): lax.dot_general(dpred, weight, (((0,), (1,)), ((), ())), preferred_elemen...  2.05 us
    all_to_all x1, waiting for transfers between devices, exchange(): lax.all_to_all(x, axes, 0, 0, axis_index_groups=[places(axes, first)], ti...  1.94 us
    unnamed x13, local copies, waits for them, and re-layouts  1.82 us
  transfers between devices with their start and end apart: 1, of which 1 were waited for; matrix products, arithmetic and copies ran while one was open for 3% of the time, Pallas kernels for 0%

profile of v5, /device:TPU:1, one launch (start us, length us, event | category | flops | bytes accessed | tf_op | source)
XLA Modules:
  0.0 79.2 jit_solution(262561237246787427)
XLA Ops:
  0.6 0.0 copy-start.2
  0.6 0.0 copy-start
  0.7 1.2 %copy.38 = f32[13,8,8,128]{3,2,1,0:T(8,128)S(1)} copy(f32[13,8,8,128]{3,1,2,0:T(8,128)} %bitcast.56) | data formatting | bytes 851968
  1.9 0.1 copy.46
  2.0 0.0 copy-done.2
  2.1 0.4 copy-done
  2.5 0.0 copy-start.1
  2.5 0.8 %shard_map.67 = f32[8,100,128]{2,1,0:T(8,128)S(1)} custom-call(bf16[1024,1024]{1,0:T(8,128)(2,1)S(1)} %bitcast.45, bf16[128,1024]{1,0:T(8,128)(2,1)S(1)} %pad.4.weight, f32[8,100,128]{2,1,0:T(8,128)S(1)} %bitcast.46), custom_call_target="tpu_custom_call" | custom-call | tf_op jit(solution)/shard_map/pallas_call | solution.py:55
  3.4 11.2 %all_to_all.25 = f16[8,100,128]{2,1,0:T(8,128)(2,1)S(1)} all-to-all(f16[8,100,128]{2,1,0:T(8,128)(2,1)S(1)} %convert_element_type.48), channel_id=1, replica_groups={{6,7,4,5,2,3,0,1},{14,15,12,13,10,11,8,9},{22,23,20,21,18,19,16,17},{30..., dimensions={0} | all-to-all | bytes 409600 | tf_op jit(solution)/shard_map/all_to_all | solution.py:38
  14.6 0.0 copy-done.1
  14.6 0.6 shard_map.68
  15.3 9.6 %all_to_all.26 = bf16[8,100,128]{2,1,0:T(8,128)(2,1)S(1)} all-to-all(bf16[8,100,128]{2,1,0:T(8,128)(2,1)S(1)} %get-tuple-element.15), channel_id=1, replica_groups={{6,7,4,5,2,3,0,1},{14,15,12,13,10,11,8,9},{22,23,20,21,18,19,16,17},{30..., dimensions={0} | all-to-all | bytes 409600 | tf_op jit(solution)/shard_map/all_to_all | solution.py:38
  25.0 0.5 fusion
  25.5 0.1 copy.40
  25.7 0.1 pad_maximum_fusion
  25.7 0.3 copy.34
  26.0 18.7 %all_to_all.27 = f16[32,13,2,128]{3,2,1,0:T(2,128)(2,1)S(1)} all-to-all(f16[32,13,2,128]{3,2,1,0:T(2,128)(2,1)S(1)} %copy.34), channel_id=1, replica_groups={{270,262,271,263,268,260,269,261,14,6,15,7,12,4,13,5,266,258,267,259,26..., dimensions={0} | all-to-all | bytes 425984 | tf_op jit(solution)/shard_map/all_to_all | solution.py:38
  44.7 0.2 convert_reduce_fusion
  44.9 0.1 broadcast_in_dim.32
  45.0 19.2 %all_to_all.28 = f16[16,13,2,128]{3,2,1,0:T(2,128)(2,1)S(1)} all-to-all(f16[16,13,2,128]{3,2,1,0:T(2,128)(2,1)S(1)} %broadcast_in_dim.32), channel_id=1, replica_groups={{128,144,160,176,192,208,224,240,0,16,32,48,64,80,96,112},{129,145,161,..., dimensions={0} | all-to-all | bytes 212992 | tf_op jit(solution)/shard_map/all_to_all | solution.py:38
  64.2 0.1 convert_reduce_fusion.1
  64.2 0.8 %broadcast_in_dim.33 = f16[32,13,2,128]{3,2,1,0:T(2,128)(2,1)} broadcast(f16[13,2,128]{2,1,0:T(2,128)(2,1)S(1)} %multiply_convert_fusion), dimensions={1,2,3} | broadcast | bytes 219648 | tf_op jit(solution)/shard_map/broadcast_in_dim | solution.py:175
  65.0 9.0 %all-to-all-start.4 = ((f16[32,13,2,128]{3,2,1,0:T(2,128)(2,1)}), f16[32,13,2,128]{3,2,1,0:T(2,128)(2,1)S(1)}, u32[]{:S(2)}, u32[]{:S(2)}) async-start(f16[32,13,2,128]{3,2,1,0:T(2,128)(2,1)} %broadcast_in_dim.33), calls=%async_computation.4 | async-start | bytes 425984 | tf_op jit(solution)/shard_map/all_to_all | solution.py:38
  74.0 2.1 %convert_bitcast_fusion = bf16[1,1024,1024]{2,1,0:T(8,128)(2,1)} fusion(bf16[100,1024]{1,0:T(8,128)(2,1)S(1)} %bitcast.49, bf16[1024,100]{0,1:T(8,128)(2,1)S(1)} %copy-done.2), kind=kOutput, calls=%fused_computation | convolution fusion | flops 210763776 | bytes 2506752 | tf_op jit(solution)/shard_map/dot_general | solution.py:160
  76.1 1.9 %all-to-all-done.4 = f16[32,13,2,128]{3,2,1,0:T(2,128)(2,1)S(1)} async-done(((f16[32,13,2,128]{3,2,1,0:T(2,128)(2,1)}), f16[32,13,2,128]{3,2,1,0:T(2,128)(2,1)S(1)}, u32[]{:S(2)}, u32[]{:S(2)}) %all-to-all-start.4) | async-done | bytes 213024 | tf_op jit(solution)/shard_map/all_to_all | solution.py:38
  78.0 0.1 copy.36
  78.1 0.1 bitcast_convert_fusion
  78.1 0.3 copy.37.refs_0_
  78.4 0.8 %shard_map.69 = (f32[100,1024]{1,0:T(8,128)}, f32[1,1]{1,0:T(1,128)}) custom-call(f32[32,26,128]{2,1,0:T(8,128)S(1)} %copy.37.refs_0_), custom_call_target="tpu_custom_call" | custom-call | tf_op jit(solution)/shard_map/pallas_call | solution.py:123
  (17 shorter events, 0.3 us)
Async XLA Ops:
  0.6 1.4 %copy-start.2 = (bf16[1024,100]{0,1:T(8,128)(2,1)S(1)}, bf16[1024,100]{0,1:T(8,128)(2,1)}, u32[]{:S(2)}) copy-start(bf16[1024,100]{0,1:T(8,128)(2,1)} %param.5) | copy-start | bytes 614404
  0.6 1.8 %copy-start = (bf16[1,1024,1024]{2,1,0:T(8,128)(2,1)S(1)}, bf16[1,1024,1024]{2,1,0:T(8,128)(2,1)}, u32[]{:S(2)}) copy-start(bf16[1,1024,1024]{2,1,0:T(8,128)(2,1)} %param.4) | copy-start | bytes 6291460
  2.5 12.1 %copy-start.1 = (f32[1024]{0:T(1024)S(1)}, f32[1024]{0:T(1024)}, u32[]{:S(2)}) copy-start(f32[1024]{0:T(1024)} %param.7) | copy-start | bytes 12292
  65.0 13.0 %all-to-all-start.4 = ((f16[32,13,2,128]{3,2,1,0:T(2,128)(2,1)}), f16[32,13,2,128]{3,2,1,0:T(2,128)(2,1)S(1)}, u32[]{:S(2)}, u32[]{:S(2)}) async-start(f16[32,13,2,128]{3,2,1,0:T(2,128)(2,1)} %broadcast_in_dim.33), calls=%async_computation.4 | async-start | bytes 425984 | tf_op jit(solution)/shard_map/all_to_all | solution.py:38

commit v6 on v5

--- a/solution.py
+++ b/solution.py
@@ -107,16 +107,26 @@
     )(rank, diff, area)
 
 
-def finish_kernel(factor, loss_factor, table, grads, loss):
+def finish_kernel(factor, loss_factor, table, grads, loss, ready, sems):
     columns = grads.shape[1] // BLOCK
+    half = V // 2 // 16 * 16
+    copies = [
+        pltpu.make_async_copy(ready.at[:half], grads.at[:half], sems.at[0]),
+        pltpu.make_async_copy(ready.at[half:], grads.at[half:], sems.at[1]),
+    ]
     for g in range(GROUPS):
         for c in range(columns):
             piece = table[g * columns + c] * factor
             lanes = slice(c * BLOCK, (c + 1) * BLOCK)
-            grads[24 * g : 24 * (g + 1), lanes] = piece[:24]
-            grads[V - GROUPS + g : V - GROUPS + g + 1, lanes] = piece[24:25]
+            ready[24 * g : 24 * (g + 1), lanes] = piece[:24]
+            ready[V - GROUPS + g : V - GROUPS + g + 1, lanes] = piece[24:25]
+        if 24 * (g + 1) == half:
+            copies[0].start()
+    copies[1].start()
     lanes = table[0, 25:26, :] + table[1, 25:26, :] * (1.0 / 1024.0)
     loss[0, 0] = jnp.sum(lanes) * loss_factor
+    copies[0].wait()
+    copies[1].wait()
 
 
 def finish(table, factor, loss_factor, width):
@@ -127,7 +137,8 @@
             jax.ShapeDtypeStruct((1, 1), jnp.float32),
         ),
         in_specs=[VMEM],
-        out_specs=(pl.BlockSpec((V, width), lambda: (0, 0)), SMEM),
+        out_specs=(pl.BlockSpec(memory_space=pltpu.HBM), SMEM),
+        scratch_shapes=[pltpu.VMEM((V, width), jnp.float32), pltpu.SemaphoreType.DMA((2,))],
         compiler_params=pltpu.CompilerParams(vmem_limit_bytes=8 * 1024 * 1024),
     )(table)
 

time: 79.6 us -> 80.1 us (level)
  no operation moved by 1% of the time
where the time goes in v6:
time: 80.1 us; the launch traced here: 79.7 us
  blocking collectives  58.7 us (73%)
  starting transfers between devices  8.97 us (11%)
  local copies, waits for them, and re-layouts  3.46 us (4%)
  Pallas kernels  2.77 us (3%)
  matrix products  2.52 us (3%)
  waiting for transfers between devices  1.94 us (2%)
  between operations  0.9 us (1%)
    all_to_all x4, blocking collectives, exchange(): lax.all_to_all(x, axes, 0, 0, axis_index_groups=[places(axes, first)], ti...  58.7 us
    all_to_all x1, starting transfers between devices, exchange(): lax.all_to_all(x, axes, 0, 0, axis_index_groups=[places(axes, first)], ti...  8.97 us
    dot_general x1, matrix products, shards(): lax.dot_general(dpred, weight, (((0,), (1,)), ((), ())), preferred_elemen...  2.05 us
    all_to_all x1, waiting for transfers between devices, exchange(): lax.all_to_all(x, axes, 0, 0, axis_index_groups=[places(axes, first)], ti...  1.94 us
    unnamed x13, local copies, waits for them, and re-layouts  1.82 us
  transfers between devices with their start and end apart: 1, of which 1 were waited for; matrix products, arithmetic and copies ran while one was open for 3% of the time, Pallas kernels for 0%

profile of v6, /device:TPU:1, one launch (start us, length us, event | category | flops | bytes accessed | tf_op | source)
XLA Modules:
  0.0 79.7 jit_solution(3442963543585766101)
XLA Ops:
  0.6 0.0 copy-start.2
  0.6 0.0 copy-start
  0.7 1.2 %copy.38 = f32[13,8,8,128]{3,2,1,0:T(8,128)S(1)} copy(f32[13,8,8,128]{3,1,2,0:T(8,128)} %bitcast.56) | data formatting | bytes 851968
  1.9 0.1 copy.46
  2.0 0.0 copy-done.2
  2.1 0.4 copy-done
  2.5 0.0 copy-start.1
  2.5 0.8 %shard_map.67 = f32[8,100,128]{2,1,0:T(8,128)S(1)} custom-call(bf16[1024,1024]{1,0:T(8,128)(2,1)S(1)} %bitcast.45, bf16[128,1024]{1,0:T(8,128)(2,1)S(1)} %pad.4.weight, f32[8,100,128]{2,1,0:T(8,128)S(1)} %bitcast.46), custom_call_target="tpu_custom_call" | custom-call | tf_op jit(solution)/shard_map/pallas_call | solution.py:55
  3.4 11.2 %all_to_all.25 = f16[8,100,128]{2,1,0:T(8,128)(2,1)S(1)} all-to-all(f16[8,100,128]{2,1,0:T(8,128)(2,1)S(1)} %convert_element_type.48), channel_id=1, replica_groups={{6,7,4,5,2,3,0,1},{14,15,12,13,10,11,8,9},{22,23,20,21,18,19,16,17},{30..., dimensions={0} | all-to-all | bytes 409600 | tf_op jit(solution)/shard_map/all_to_all | solution.py:38
  14.6 0.0 copy-done.1
  14.6 0.6 shard_map.68
  15.3 9.6 %all_to_all.26 = bf16[8,100,128]{2,1,0:T(8,128)(2,1)S(1)} all-to-all(bf16[8,100,128]{2,1,0:T(8,128)(2,1)S(1)} %get-tuple-element.15), channel_id=1, replica_groups={{6,7,4,5,2,3,0,1},{14,15,12,13,10,11,8,9},{22,23,20,21,18,19,16,17},{30..., dimensions={0} | all-to-all | bytes 409600 | tf_op jit(solution)/shard_map/all_to_all | solution.py:38
  25.0 0.5 fusion
  25.5 0.1 copy.40
  25.7 0.1 pad_maximum_fusion
  25.7 0.3 copy.34
  26.0 18.7 %all_to_all.27 = f16[32,13,2,128]{3,2,1,0:T(2,128)(2,1)S(1)} all-to-all(f16[32,13,2,128]{3,2,1,0:T(2,128)(2,1)S(1)} %copy.34), channel_id=1, replica_groups={{270,262,271,263,268,260,269,261,14,6,15,7,12,4,13,5,266,258,267,259,26..., dimensions={0} | all-to-all | bytes 425984 | tf_op jit(solution)/shard_map/all_to_all | solution.py:38
  44.7 0.2 convert_reduce_fusion
  44.9 0.1 broadcast_in_dim.32
  45.0 19.2 %all_to_all.28 = f16[16,13,2,128]{3,2,1,0:T(2,128)(2,1)S(1)} all-to-all(f16[16,13,2,128]{3,2,1,0:T(2,128)(2,1)S(1)} %broadcast_in_dim.32), channel_id=1, replica_groups={{128,144,160,176,192,208,224,240,0,16,32,48,64,80,96,112},{129,145,161,..., dimensions={0} | all-to-all | bytes 212992 | tf_op jit(solution)/shard_map/all_to_all | solution.py:38
  64.2 0.1 convert_reduce_fusion.1
  64.2 0.8 broadcast_in_dim.33
  65.0 9.0 %all-to-all-start.4 = ((f16[32,13,2,128]{3,2,1,0:T(2,128)(2,1)}), f16[32,13,2,128]{3,2,1,0:T(2,128)(2,1)S(1)}, u32[]{:S(2)}, u32[]{:S(2)}) async-start(f16[32,13,2,128]{3,2,1,0:T(2,128)(2,1)} %broadcast_in_dim.33), calls=%async_computation.4 | async-start | bytes 425984 | tf_op jit(solution)/shard_map/all_to_all | solution.py:38
  74.0 2.1 %convert_bitcast_fusion = bf16[1,1024,1024]{2,1,0:T(8,128)(2,1)} fusion(bf16[100,1024]{1,0:T(8,128)(2,1)S(1)} %bitcast.49, bf16[1024,100]{0,1:T(8,128)(2,1)S(1)} %copy-done.2), kind=kOutput, calls=%fused_computation | convolution fusion | flops 210763776 | bytes 2506752 | tf_op jit(solution)/shard_map/dot_general | solution.py:171
  76.1 1.9 %all-to-all-done.4 = f16[32,13,2,128]{3,2,1,0:T(2,128)(2,1)S(1)} async-done(((f16[32,13,2,128]{3,2,1,0:T(2,128)(2,1)}), f16[32,13,2,128]{3,2,1,0:T(2,128)(2,1)S(1)}, u32[]{:S(2)}, u32[]{:S(2)}) %all-to-all-start.4) | async-done | bytes 213024 | tf_op jit(solution)/shard_map/all_to_all | solution.py:38
  78.0 0.1 copy.36
  78.1 0.1 bitcast_convert_fusion
  78.1 0.3 copy.37.refs_0_
  78.4 1.3 %shard_map.69 = (f32[100,1024]{1,0:T(8,128)}, f32[1,1]{1,0:T(1,128)}) custom-call(f32[32,26,128]{2,1,0:T(8,128)S(1)} %copy.37.refs_0_), custom_call_target="tpu_custom_call" | custom-call | tf_op jit(solution)/shard_map/pallas_call | solution.py:133
  (17 shorter events, 0.3 us)
Async XLA Ops:
  0.6 1.4 %copy-start.2 = (bf16[1024,100]{0,1:T(8,128)(2,1)S(1)}, bf16[1024,100]{0,1:T(8,128)(2,1)}, u32[]{:S(2)}) copy-start(bf16[1024,100]{0,1:T(8,128)(2,1)} %param.5) | copy-start | bytes 614404
  0.6 1.8 %copy-start = (bf16[1,1024,1024]{2,1,0:T(8,128)(2,1)S(1)}, bf16[1,1024,1024]{2,1,0:T(8,128)(2,1)}, u32[]{:S(2)}) copy-start(bf16[1,1024,1024]{2,1,0:T(8,128)(2,1)} %param.4) | copy-start | bytes 6291460
  2.5 12.1 %copy-start.1 = (f32[1024]{0:T(1024)S(1)}, f32[1024]{0:T(1024)}, u32[]{:S(2)}) copy-start(f32[1024]{0:T(1024)} %param.7) | copy-start | bytes 12292
  65.0 13.0 %all-to-all-start.4 = ((f16[32,13,2,128]{3,2,1,0:T(2,128)(2,1)}), f16[32,13,2,128]{3,2,1,0:T(2,128)(2,1)S(1)}, u32[]{:S(2)}, u32[]{:S(2)}) async-start(f16[32,13,2,128]{3,2,1,0:T(2,128)(2,1)} %broadcast_in_dim.33), calls=%async_computation.4 | async-start | bytes 425984 | tf_op jit(solution)/shard_map/all_to_all | solution.py:38

commit v7 on v5

--- a/solution.py
+++ b/solution.py
@@ -15,7 +15,8 @@
 GRID = ("y_lo", "z", "core")
 PLANE = ("y_hi", "y_lo", "x", "core")
 MEMBER_FIRST = (1, 2)
-PLANE_FIRST = (1, 1, 2, 1)
+SUM_FIRST = (1, 1, 2, 1)
+COPY_FIRST = (1, 0, 2, 1)
 Z_FIRST = (8,)
 WSCALE = 0.25
 LSCALE = 1.0 / 512.0
@@ -107,21 +108,21 @@
     )(rank, diff, area)
 
 
-def finish_kernel(factor, loss_factor, table, grads, loss):
+def finish_kernel(spots, factor, loss_factor, table, grads, loss):
     columns = grads.shape[1] // BLOCK
     for g in range(GROUPS):
         for c in range(columns):
-            piece = table[g * columns + c] * factor
+            piece = table[spots[g * columns + c]] * factor
             lanes = slice(c * BLOCK, (c + 1) * BLOCK)
             grads[24 * g : 24 * (g + 1), lanes] = piece[:24]
             grads[V - GROUPS + g : V - GROUPS + g + 1, lanes] = piece[24:25]
-    lanes = table[0, 25:26, :] + table[1, 25:26, :] * (1.0 / 1024.0)
+    lanes = table[spots[0], 25:26, :] + table[spots[1], 25:26, :] * (1.0 / 1024.0)
     loss[0, 0] = jnp.sum(lanes) * loss_factor
 
 
-def finish(table, factor, loss_factor, width):
+def finish(table, spots, factor, loss_factor, width):
     return pl.pallas_call(
-        lambda *refs: finish_kernel(factor, loss_factor, *refs),
+        lambda *refs: finish_kernel(spots, factor, loss_factor, *refs),
         out_shape=(
             jax.ShapeDtypeStruct((V, width), jnp.float32),
             jax.ShapeDtypeStruct((1, 1), jnp.float32),
@@ -167,16 +168,19 @@
     body = wterm[: V - GROUPS].reshape(GROUPS, 24, columns, BLOCK).transpose(0, 2, 1, 3)
     last = wterm[V - GROUPS :].reshape(GROUPS, columns, 1, BLOCK)
     chunks = jnp.concatenate([body, last, spare], axis=2).reshape(plane, 13, 2, BLOCK)
-    mine = jnp.sum(exchange(chunks, PLANE, PLANE_FIRST).astype(jnp.float32), axis=0)
+    mine = jnp.sum(exchange(chunks, PLANE, SUM_FIRST).astype(jnp.float32), axis=0)
     mine = (mine * (1.0 / plane)).astype(jnp.float16)
     ring = exchange(jnp.broadcast_to(mine[None], (depth, 13, 2, BLOCK)), ("z",), Z_FIRST)
     mine = jnp.sum(ring.astype(jnp.float32), axis=0)
     mine = (mine * (1.0 / depth)).astype(jnp.float16)
-    whole = exchange(jnp.broadcast_to(mine[None], (plane, 13, 2, BLOCK)), PLANE, PLANE_FIRST)
+    whole = exchange(jnp.broadcast_to(mine[None], (plane, 13, 2, BLOCK)), PLANE, COPY_FIRST)
     whole = whole.reshape(plane, 26, BLOCK)
     devices = plane * depth
+    copied = places(PLANE, COPY_FIRST)
+    spots = [copied.index(device) for device in places(PLANE, SUM_FIRST)]
     grads, total = finish(
         whole.astype(jnp.float32),
+        spots,
         devices / WSCALE / grid_total,
         devices / LSCALE / (grid_total * V * members),
         width,

time: 79.6 us -> 79.4 us (level)
  no operation moved by 1% of the time
where the time goes in v7:
time: 79.4 us; the launch traced here: 79.1 us
  blocking collectives  58.7 us (74%)
  starting transfers between devices  9.08 us (11%)
  local copies, waits for them, and re-layouts  3.46 us (4%)
  matrix products  2.52 us (3%)
  Pallas kernels  2.27 us (3%)
  waiting for transfers between devices  1.69 us (2%)
  between operations  0.9 us (1%)
    all_to_all x4, blocking collectives, exchange(): lax.all_to_all(x, axes, 0, 0, axis_index_groups=[places(axes, first)], ti...  58.7 us
    all_to_all x1, starting transfers between devices, exchange(): lax.all_to_all(x, axes, 0, 0, axis_index_groups=[places(axes, first)], ti...  9.08 us
    dot_general x1, matrix products, shards(): lax.dot_general(dpred, weight, (((0,), (1,)), ((), ())), preferred_elemen...  2.05 us
    unnamed x13, local copies, waits for them, and re-layouts  1.82 us
    all_to_all x1, waiting for transfers between devices, exchange(): lax.all_to_all(x, axes, 0, 0, axis_index_groups=[places(axes, first)], ti...  1.69 us
  transfers between devices with their start and end apart: 1, of which 1 were waited for; matrix products, arithmetic and copies ran while one was open for 3% of the time, Pallas kernels for 0%

profile of v7, /device:TPU:1, one launch (start us, length us, event | category | flops | bytes accessed | tf_op | source)
XLA Modules:
  0.0 79.1 jit_solution(8027572849417322825)
XLA Ops:
  0.6 0.0 copy-start.2
  0.6 0.0 copy-start
  0.7 1.2 %copy.38 = f32[13,8,8,128]{3,2,1,0:T(8,128)S(1)} copy(f32[13,8,8,128]{3,1,2,0:T(8,128)} %bitcast.56) | data formatting | bytes 851968
  1.9 0.1 copy.46
  2.0 0.0 copy-done.2
  2.1 0.4 copy-done
  2.5 0.0 copy-start.1
  2.5 0.8 %shard_map.67 = f32[8,100,128]{2,1,0:T(8,128)S(1)} custom-call(bf16[1024,1024]{1,0:T(8,128)(2,1)S(1)} %bitcast.45, bf16[128,1024]{1,0:T(8,128)(2,1)S(1)} %pad.4.weight, f32[8,100,128]{2,1,0:T(8,128)S(1)} %bitcast.46), custom_call_target="tpu_custom_call" | custom-call | tf_op jit(solution)/shard_map/pallas_call | solution.py:56
  3.4 11.2 %all_to_all.25 = f16[8,100,128]{2,1,0:T(8,128)(2,1)S(1)} all-to-all(f16[8,100,128]{2,1,0:T(8,128)(2,1)S(1)} %convert_element_type.48), channel_id=1, replica_groups={{6,7,4,5,2,3,0,1},{14,15,12,13,10,11,8,9},{22,23,20,21,18,19,16,17},{30..., dimensions={0} | all-to-all | bytes 409600 | tf_op jit(solution)/shard_map/all_to_all | solution.py:39
  14.6 0.0 copy-done.1
  14.6 0.6 shard_map.68
  15.3 9.6 %all_to_all.26 = bf16[8,100,128]{2,1,0:T(8,128)(2,1)S(1)} all-to-all(bf16[8,100,128]{2,1,0:T(8,128)(2,1)S(1)} %get-tuple-element.15), channel_id=1, replica_groups={{6,7,4,5,2,3,0,1},{14,15,12,13,10,11,8,9},{22,23,20,21,18,19,16,17},{30..., dimensions={0} | all-to-all | bytes 409600 | tf_op jit(solution)/shard_map/all_to_all | solution.py:39
  25.0 0.5 fusion
  25.5 0.1 copy.40
  25.7 0.1 pad_maximum_fusion
  25.7 0.3 copy.34
  26.0 18.7 %all_to_all.27 = f16[32,13,2,128]{3,2,1,0:T(2,128)(2,1)S(1)} all-to-all(f16[32,13,2,128]{3,2,1,0:T(2,128)(2,1)S(1)} %copy.34), channel_id=1, replica_groups={{270,262,271,263,268,260,269,261,14,6,15,7,12,4,13,5,266,258,267,259,26..., dimensions={0} | all-to-all | bytes 425984 | tf_op jit(solution)/shard_map/all_to_all | solution.py:39
  44.7 0.2 convert_reduce_fusion
  44.9 0.1 broadcast_in_dim.32
  45.0 19.2 %all_to_all.28 = f16[16,13,2,128]{3,2,1,0:T(2,128)(2,1)S(1)} all-to-all(f16[16,13,2,128]{3,2,1,0:T(2,128)(2,1)S(1)} %broadcast_in_dim.32), channel_id=1, replica_groups={{128,144,160,176,192,208,224,240,0,16,32,48,64,80,96,112},{129,145,161,..., dimensions={0} | all-to-all | bytes 212992 | tf_op jit(solution)/shard_map/all_to_all | solution.py:39
  64.2 0.1 convert_reduce_fusion.1
  64.2 0.8 %broadcast_in_dim.33 = f16[32,13,2,128]{3,2,1,0:T(2,128)(2,1)} broadcast(f16[13,2,128]{2,1,0:T(2,128)(2,1)S(1)} %multiply_convert_fusion), dimensions={1,2,3} | broadcast | bytes 219648 | tf_op jit(solution)/shard_map/broadcast_in_dim | solution.py:176
  65.0 9.1 %all-to-all-start.4 = ((f16[32,13,2,128]{3,2,1,0:T(2,128)(2,1)}), f16[32,13,2,128]{3,2,1,0:T(2,128)(2,1)S(1)}, u32[]{:S(2)}, u32[]{:S(2)}) async-start(f16[32,13,2,128]{3,2,1,0:T(2,128)(2,1)} %broadcast_in_dim.33), calls=%async_computation.4 | async-start | bytes 425984 | tf_op jit(solution)/shard_map/all_to_all | solution.py:39
  74.1 2.1 %convert_bitcast_fusion = bf16[1,1024,1024]{2,1,0:T(8,128)(2,1)} fusion(bf16[100,1024]{1,0:T(8,128)(2,1)S(1)} %bitcast.49, bf16[1024,100]{0,1:T(8,128)(2,1)S(1)} %copy-done.2), kind=kOutput, calls=%fused_computation | convolution fusion | flops 210763776 | bytes 2506752 | tf_op jit(solution)/shard_map/dot_general | solution.py:161
  76.2 1.7 %all-to-all-done.4 = f16[32,13,2,128]{3,2,1,0:T(2,128)(2,1)S(1)} async-done(((f16[32,13,2,128]{3,2,1,0:T(2,128)(2,1)}), f16[32,13,2,128]{3,2,1,0:T(2,128)(2,1)S(1)}, u32[]{:S(2)}, u32[]{:S(2)}) %all-to-all-start.4) | async-done | bytes 213024 | tf_op jit(solution)/shard_map/all_to_all | solution.py:39
  77.9 0.1 copy.36
  77.9 0.1 bitcast_convert_fusion
  78.0 0.3 copy.37.refs_0_
  78.3 0.8 %shard_map.69 = (f32[100,1024]{1,0:T(8,128)}, f32[1,1]{1,0:T(1,128)}) custom-call(f32[32,26,128]{2,1,0:T(8,128)S(1)} %copy.37.refs_0_), custom_call_target="tpu_custom_call" | custom-call | tf_op jit(solution)/shard_map/pallas_call | solution.py:124
  (17 shorter events, 0.3 us)
Async XLA Ops:
  0.6 1.4 %copy-start.2 = (bf16[1024,100]{0,1:T(8,128)(2,1)S(1)}, bf16[1024,100]{0,1:T(8,128)(2,1)}, u32[]{:S(2)}) copy-start(bf16[1024,100]{0,1:T(8,128)(2,1)} %param.5) | copy-start | bytes 614404
  0.6 1.8 %copy-start = (bf16[1,1024,1024]{2,1,0:T(8,128)(2,1)S(1)}, bf16[1,1024,1024]{2,1,0:T(8,128)(2,1)}, u32[]{:S(2)}) copy-start(bf16[1,1024,1024]{2,1,0:T(8,128)(2,1)} %param.4) | copy-start | bytes 6291460
  2.5 12.1 %copy-start.1 = (f32[1024]{0:T(1024)S(1)}, f32[1024]{0:T(1024)}, u32[]{:S(2)}) copy-start(f32[1024]{0:T(1024)} %param.7) | copy-start | bytes 12292
  65.0 12.8 %all-to-all-start.4 = ((f16[32,13,2,128]{3,2,1,0:T(2,128)(2,1)}), f16[32,13,2,128]{3,2,1,0:T(2,128)(2,1)S(1)}, u32[]{:S(2)}, u32[]{:S(2)}) async-start(f16[32,13,2,128]{3,2,1,0:T(2,128)(2,1)} %broadcast_in_dim.33), calls=%async_computation.4 | async-start | bytes 425984 | tf_op jit(solution)/shard_map/all_to_all | solution.py:39
